TPU v7x, 256 devices: a whole 4x4x8 slice. The times are simulated.
256 devices in a mesh: sec: 64 (over z, x, core), blk: 4 (over y).
Axes of the slice: x: 4, y: 4, z: 8, core: 2. Of those that a mesh axis runs over, the one named last changes fastest.
Arguments:
- state: float32 [8, 16384, 2048], P(None, 'sec', 'blk'), may hold values from -6 to 6
- velocity: float32 [2, 16384, 2048], P(None, 'sec', 'blk'), may hold values from -1 to 1
- limiter: int32 [16384, 2048], P('sec', 'blk'), may hold values from 0 to 1
- footpoint_owner: int32 [64, 4, 1024, 1], P('sec', 'blk'), may hold values from 0 to 63; in each aligned block of 1024 rows (0 to 1023, 1024 to 2047, ..., all dimensions but the last counted through in order) at most 32 rows name the same one
- footpoint_slot: int32 [64, 4, 1024, 1], P('sec', 'blk'), may hold values from 0 to 63
- conductance: float32 [1024, 2048], P('sec', 'blk'), may hold values from 1 to 10
- potential_prior: float32 [1024, 2048], P('sec', 'blk'), may hold values from -6 to 6
Outputs:
- new_state: float32 [8, 16384, 2048], P(None, 'sec', 'blk')
- shell_potential: float32 [1024, 2048], P('sec', 'blk')
- foot_potential: float32 [16384, 2048], P('sec', 'blk')
Inputs may be any that keep to these rules, and one draw needn't show every extreme that they name: `footpoint_owner`: among the 1024 blocks of one device no section is named more than 32 times, a bound that some block reaches.
All inputs are finite; a program needn't handle non-finite values.
Results may differ from a plain program's by a relative error of at most 0.0003.
Values sent between devices are 32-bit elements; how exact they have to be, the bound alone decides.
A program may use at most 128 MiB of HBM per device.

v0:
```python
import jax
import jax.numpy as jnp
from jax import lax
from jax.sharding import PartitionSpec as P

ITERS = 4


courant = 0.4
leak = 1.0


def with_halo(shard, sides, width, wrap):
    for axis, dim in sides:
        size, length = (lax.axis_size(axis), shard.shape[dim])
        up = [(i, (i + 1) % size) for i in range(size if wrap else size - 1)]
        down = [(j, i) for i, j in up]
        last = lax.slice_in_dim(shard, length - width, length, axis=dim)
        leading = lax.slice_in_dim(shard, 0, width, axis=dim)
        before = lax.ppermute(last, axis, up)
        after = lax.ppermute(leading, axis, down)
        shard = jnp.concatenate([before, shard, after], axis=dim)
    return shard


def minmod(lower_diff, upper_diff):
    return jnp.where(
        lower_diff * upper_diff > 0.0,
        jnp.sign(lower_diff) * jnp.minimum(jnp.abs(lower_diff), jnp.abs(upper_diff)),
        0.0,
    )


def window(array, off_x, off_y):
    return array[
        ..., 2 + off_x : array.shape[-2] - 2 + off_x, 2 + off_y : array.shape[-1] - 2 + off_y
    ]


def flux_change(field, speed, weight, along_x):

    def shifted(array, offset):
        return window(array, offset, 0) if along_x else window(array, 0, offset)

    slopes = [
        shifted(weight, offset)
        * minmod(
            shifted(field, offset) - shifted(field, offset - 1),
            shifted(field, offset + 1) - shifted(field, offset),
        )
        for offset in (-1, 0, 1)
    ]
    fluxes = []
    for offset in (-1, 0):
        left_value = shifted(field, offset) + 0.5 * slopes[offset + 1]
        right_value = shifted(field, offset + 1) - 0.5 * slopes[offset + 2]
        face_speed = 0.5 * (shifted(speed, offset) + shifted(speed, offset + 1))
        fluxes.append(
            jnp.where(face_speed > 0.0, face_speed * left_value, face_speed * right_value)
        )
    return fluxes[1] - fluxes[0]


def advance(field, speed_x, speed_y, weight):
    return window(field, 0, 0) - courant * (
        flux_change(field, speed_x, weight, True) + flux_change(field, speed_y, weight, False)
    )


def curl_field(padded):
    field_x = padded[0]
    field_y = padded[1]
    return 0.5 * (field_y[2:, 1:-1] - field_y[:-2, 1:-1]) - 0.5 * (
        field_x[1:-1, 2:] - field_x[1:-1, :-2]
    )


def relax(potential_ext, sigma_ext, source):
    centre = sigma_ext[1:-1, 1:-1]
    north = 0.5 * (centre + sigma_ext[:-2, 1:-1])
    south = 0.5 * (centre + sigma_ext[2:, 1:-1])
    west = 0.5 * (centre + sigma_ext[1:-1, :-2])
    east = 0.5 * (centre + sigma_ext[1:-1, 2:])
    total = (
        north * potential_ext[:-2, 1:-1]
        + south * potential_ext[2:, 1:-1]
        + west * potential_ext[1:-1, :-2]
        + east * potential_ext[1:-1, 2:]
        + source
    )
    return total / (north + south + west + east + leak)


def cropped(array, depth, keep):
    cut = depth - keep
    return array[cut : array.shape[0] - cut, cut : array.shape[1] - cut]


def on_device(
    state, velocity, limiter, footpoint_owner, footpoint_slot, conductance, potential_prior
):
    quantities = state.shape[0]
    rows_x = state.shape[1]
    rows_y = state.shape[2]
    stacked = jnp.concatenate([state, velocity, limiter.astype(jnp.float32)[None]], axis=0)
    extended = with_halo(stacked, (("sec", 1), ("blk", 2)), 2, True)
    new_state = advance(
        extended[:quantities],
        extended[quantities],
        extended[quantities + 1],
        extended[quantities + 2],
    )
    fields = with_halo(new_state[quantities - 2 :], (("sec", 1), ("blk", 2)), 1, True)
    current = curl_field(fields)
    sections = lax.axis_size("sec")
    num_blocks = rows_x * rows_y // 128
    capacity = max(2, 2 * num_blocks // sections)
    blocks = current.reshape(num_blocks, 128)
    owner = footpoint_owner.reshape(num_blocks)
    slot = footpoint_slot.reshape(num_blocks)
    onehot = (owner[:, None] == jnp.arange(sections, dtype=jnp.int32)[None, :]).astype(jnp.int32)
    before = jnp.cumsum(onehot, axis=0) - onehot
    place = jnp.sum(before * onehot, axis=1)
    flat_index = owner * capacity + place
    send_blocks = jnp.zeros((sections * capacity, 128), jnp.float32).at[flat_index].set(blocks)
    send_slots = (
        jnp.full((sections * capacity,), -1.0, jnp.float32)
        .at[flat_index]
        .set(slot.astype(jnp.float32))
    )
    got_blocks, got_slots = (
        lax.all_to_all(
            send_blocks.reshape(sections, capacity, 128),
            "sec",
            split_axis=0,
            concat_axis=0,
            tiled=True,
        ),
        lax.all_to_all(
            send_slots.reshape(sections, capacity), "sec", split_axis=0, concat_axis=0, tiled=True
        ),
    )
    lat_rows = conductance.shape[0]
    lon_cols = conductance.shape[1]
    shell_blocks = lat_rows * lon_cols // 128
    got_flat = got_slots.reshape(sections * capacity)
    selector = (got_flat[:, None] == jnp.arange(shell_blocks, dtype=jnp.float32)[None, :]).astype(
        jnp.float32
    )
    source_blocks = jnp.dot(
        selector.T,
        got_blocks.reshape(sections * capacity, 128),
        precision=lax.Precision.HIGHEST,
        preferred_element_type=jnp.float32,
    )
    source = source_blocks.reshape(lat_rows, lon_cols)
    depth = 2
    shell_ext = with_halo(
        jnp.stack([conductance, source, potential_prior]), (("sec", 1), ("blk", 2)), depth, False
    )
    sigma_deep = shell_ext[0]
    source_deep = shell_ext[1]
    prior_deep = shell_ext[2]
    potential = relax(
        cropped(prior_deep, depth, 1), cropped(sigma_deep, depth, 1), cropped(source_deep, depth, 0)
    )
    for step in range(1, ITERS):
        padded = with_halo(potential, (("sec", 0), ("blk", 1)), 1, False)
        potential = relax(padded, cropped(sigma_deep, depth, 1), cropped(source_deep, depth, 0))
    table = potential.reshape(shell_blocks, 128)
    picked = table[jnp.maximum(got_flat, 0.0).astype(jnp.int32)]
    back = lax.all_to_all(
        picked.reshape(sections, capacity, 128), "sec", split_axis=0, concat_axis=0, tiled=True
    )
    foot_blocks = back.reshape(sections * capacity, 128)[flat_index]
    foot_potential = foot_blocks.reshape(rows_x, rows_y)
    return (new_state, potential, foot_potential)


def solution(mesh):
    in_specs = (
        P(None, "sec", "blk"),
        P(None, "sec", "blk"),
        P("sec", "blk"),
        P("sec", "blk", None, None),
        P("sec", "blk", None, None),
        P("sec", "blk"),
        P("sec", "blk"),
    )
    out_specs = (P(None, "sec", "blk"), P("sec", "blk"), P("sec", "blk"))
    return jax.shard_map(
        on_device, mesh=mesh, in_specs=in_specs, out_specs=out_specs, check_vma=False
    )
```

profile of v0, /device:TPU:1, one launch (start us, length us, event | category | flops | bytes accessed | tf_op | source)
XLA Modules:
  0.0 282.2 jit_solution(16465119851299491349)
XLA Ops:
  0.6 1.1 convert_bitcast_fusion
  1.7 1.1 pad_maximum_fusion.20
  2.9 2.7 collective-permute-start
  5.6 0.7 collective-permute-start.1
  6.3 18.0 %reduce-window.6 = s32[64,8,128]{2,1,0:T(8,128)S(1)} reduce-window(s32[64,8,128]{2,1,0:T(8,128)S(1)} %fusion.17, s32[]{:T(128)} %constant.14.clone.1), window={size=1x1x128 pad=0_0x0_0x127_0}, to_apply=%region_0.1 | reduce-window | flops 8323072 | bytes 524292 | tf_op jit(solution)/shard_map/reduce-window
  24.9 3.2 %pad_maximum_fusion.2 = (f32[11,260,2]{2,1,0:T(8,128)S(1)}, f32[11,260,2]{2,1,0:T(8,128)}) fusion(f32[11,2,512]{2,1,0:T(2,128)S(1)} %collective-permute-done.1, f32[11,2,512]{2,1,0:T(2,128)S(1)} %collective-permute-done, f32[1,256,512]{2,1,0:T(8,128)S(1)} %convert_bitcast_fusion, f32[2,256,512]{2,1,0:T(8,128)S(1)} %copy-done.1, f32[8,256,512]{2,1,0:T(8,128)} %param.7), kind=kLoop, calls=%fused_computation.23 | loop fusion | flops 45760 | bytes 5903040 | tf_op jit(solution)/shard_map/concatenate | solution.py:22
  28.1 2.0 copy.45
  30.1 0.6 collective-permute-start.2
  30.7 0.6 copy.46
  31.4 2.2 collective-permute-start.3
  33.5 7.4 %pad_maximum_fusion.1 = (f32[11,258,512]{2,1,0:T(8,128)}, f32[11,258,512]{2,1,0:T(8,128)}) fusion(f32[11,2,512]{2,1,0:T(2,128)S(1)} %collective-permute-done.1, f32[1,256,512]{2,1,0:T(8,128)S(1)} %convert_bitcast_fusion, f32[2,256,512]{2,1,0:T(8,128)S(1)} %copy-done.1, f32[8,256,512]{2,1,0:T(8,128)} %param.7, f32[11,2,512]{2,1,0:T(2,128)S(1)} %collective-permute-done), kind=kLoop, calls=%fused_computation.7 | loop fusion | flops 8718336 | bytes 17481728 | tf_op jit(solution)/shard_map/concatenate | solution.py:22
  40.9 0.5 copy.47
  41.4 2.4 copy.48
  43.8 1.6 maximum_bitcast_fusion.1
  45.5 2.2 fusion.65
  47.7 0.9 copy-done
  48.9 2.3 broadcast_compare_fusion.1
  51.2 12.3 %pad_maximum_fusion = (f32[11,260,514]{2,1,0:T(8,128)}, f32[11,260,514]{2,1,0:T(8,128)}) fusion(f32[11,260,2]{2,1,0:T(8,128)S(1)} %copy-done.2, f32[11,2,512]{2,1,0:T(2,128)S(1)} %collective-permute-done.1, f32[1,256,512]{2,1,0:T(8,128)S(1)} %convert_bitcast_fusion, f32[2,256,512]{2,1,0:T(8,128)S(1)} %copy-done.1, f32[8,256,512]{2,1,0:T(8,128)S(1)} %copy-done, ...), kind=kLoop, calls=%fused_computation.5 | loop fusion | flops 14700400 | bytes 17663360 | tf_op jit(solution)/shard_map/concatenate | solution.py:22
  63.6 24.2 %multiply_subtract_fusion = f32[8,256,512]{2,1,0:T(8,128)S(1)} fusion(f32[8,256,512]{2,1,0:T(8,128)S(1)} %copy-done, f32[11,260,514]{2,1,0:T(8,128)} %get-tuple-element.25, f32[11,260,514]{2,1,0:T(8,128)} %get-tuple-element.24, f32[11,258,512]{2,1,0:T(8,128)S(1)} %bitcast.57, f32[11,258,512]{2,1,0:T(8,128)S(1)} %bitcast.55, ...), kind=kLoop, calls=%fused_computation.12 | loop fusion | flops 93323264 | bytes 47185920 | tf_op jit(solution)/shard_map/sub | solution.py:65
  87.8 1.7 collective-permute-start.4
  89.5 4.8 %collective-permute-start.5 = (f32[2,1,512]{2,1,0:T(1,128)S(1)}, f32[2,1,512]{2,1,0:T(1,128)S(1)}, u32[]{:S(2)}, u32[]{:S(2)}) collective-permute-start(f32[2,1,512]{2,1,0:T(1,128)S(1)} %get-tuple-element.33), channel_id=1, source_target_pairs={{4,0},{8,4},{12,8},{16,12},{20,16},{24,20},{28,24},{32,28},{36,32}... | collective-permute-start | bytes 12296 | tf_op jit(solution)/shard_map/ppermute | solution.py:21
  94.5 0.4 collective-permute-done.4
  95.5 2.6 collective-permute-start.7
  98.1 4.3 %scatter_custom_fusion = f32[2048]{0:T(1024)S(1)} fusion(s32[1024]{0:T(1024)S(1)} %bitcast.72, f32[1024]{0:T(1024)S(1)} %bitcast.75, f32[]{:T(128)} %constant.12.clone.1), kind=kCustom, calls=%fused_computation.172 | custom fusion | bytes 8196 | tf_op jit(solution)/shard_map/scatter | solution.py:129
  102.4 0.7 all_to_all.12
  103.1 14.3 %all-to-all-start = ((f32[64,1,32]{2,1,0:T(1,128)}), f32[64,1,32]{2,1,0:T(1,128)S(1)}, u32[]{:S(2)}, u32[]{:S(2)}) async-start(f32[64,1,32]{2,1,0:T(1,128)} %bitcast.13), calls=%async_computation | async-start | bytes 65536 | tf_op jit(solution)/shard_map/all_to_all | solution.py:139
  117.5 0.5 pad_maximum_fusion.7
  118.1 0.5 fusion.5
  118.7 4.1 %scatter_custom_fusion.1 = f32[2048,128]{1,0:T(8,128)} fusion(s32[1024]{0:T(1024)S(1)} %bitcast.73, f32[1024,128]{1,0:T(8,128)S(1)} %reshape.153, f32[]{:T(128)} %constant.10.clone.1), kind=kCustom, calls=%fused_computation.55 | custom fusion | bytes 1048580 | tf_op jit(solution)/shard_map/scatter | solution.py:125
  122.8 3.9 %all-to-all-done = f32[64,1,32]{2,1,0:T(1,128)S(1)} async-done(((f32[64,1,32]{2,1,0:T(1,128)}), f32[64,1,32]{2,1,0:T(1,128)S(1)}, u32[]{:S(2)}, u32[]{:S(2)}) %all-to-all-start) | async-done | bytes 8224 | tf_op jit(solution)/shard_map/all_to_all | solution.py:139
  126.8 6.3 %all-to-all-start.1 = ((f32[64,32,128]{2,1,0:T(8,128)}), f32[64,32,128]{2,1,0:T(8,128)S(1)}, u32[]{:S(2)}, u32[]{:S(2)}) async-start(f32[64,32,128]{2,1,0:T(8,128)} %bitcast.16), calls=%async_computation.1 | async-start | bytes 2097152 | tf_op jit(solution)/shard_map/all_to_all | solution.py:132
  133.1 0.5 broadcast.140
  133.6 0.7 reduce.7
  134.4 26.7 %all-to-all-done.1 = f32[64,32,128]{2,1,0:T(8,128)S(1)} async-done(((f32[64,32,128]{2,1,0:T(8,128)}), f32[64,32,128]{2,1,0:T(8,128)S(1)}, u32[]{:S(2)}, u32[]{:S(2)}) %all-to-all-start.1) | async-done | bytes 1048608 | tf_op jit(solution)/shard_map/all_to_all | solution.py:132
  161.1 1.3 fusion.2
  162.5 4.3 %collective-permute-start.8 = (f32[3,2,512]{2,1,0:T(2,128)S(1)}, f32[3,2,512]{2,1,0:T(2,128)S(1)}, u32[]{:S(2)}, u32[]{:S(2)}) collective-permute-start(f32[3,2,512]{2,1,0:T(2,128)S(1)} %get-tuple-element.52), channel_id=1, source_target_pairs={{0,4},{4,8},{8,12},{12,16},{16,20},{20,24},{24,28},{28,32},{32,36}... | collective-permute-start | bytes 36872 | tf_op jit(solution)/shard_map/ppermute | solution.py:20
  166.8 1.9 collective-permute-start.9
  168.8 3.1 %collective-permute-done.9 = f32[3,2,512]{2,1,0:T(2,128)S(1)} collective-permute-done((f32[3,2,512]{2,1,0:T(2,128)S(1)}, f32[3,2,512]{2,1,0:T(2,128)S(1)}, u32[]{:S(2)}, u32[]{:S(2)}) %collective-permute-start.9) | collective-permute-done | bytes 12320 | tf_op jit(solution)/shard_map/ppermute | solution.py:21
  171.9 1.3 collective-permute-start.10
  173.2 1.3 collective-permute-start.11
  174.6 3.4 %collective-permute-done.11 = f32[3,20,2]{2,1,0:T(8,128)S(1)} collective-permute-done((f32[3,20,2]{2,1,0:T(8,128)S(1)}, f32[3,20,2]{2,1,0:T(8,128)S(1)}, u32[]{:S(2)}, u32[]{:S(2)}) %collective-permute-start.11) | collective-permute-done | bytes 512 | tf_op jit(solution)/shard_map/ppermute | solution.py:21
  178.3 3.1 %collective-permute-start.12 = (f32[1,512]{1,0:T(1,128)S(1)}, f32[1,512]{1,0:T(1,128)S(1)}, u32[]{:S(2)}, u32[]{:S(2)}) collective-permute-start(f32[1,512]{1,0:T(1,128)S(1)} %get-tuple-element.64), channel_id=1, source_target_pairs={{0,4},{4,8},{8,12},{12,16},{16,20},{20,24},{24,28},{28,32},{32,36}... | collective-permute-start | bytes 6152 | tf_op jit(solution)/shard_map/ppermute | solution.py:20
  181.4 1.9 collective-permute-start.13
  183.5 2.8 collective-permute-done.13
  186.4 3.0 %collective-permute-start.14 = (f32[18,1]{1,0:T(8,128)S(1)}, f32[18,1]{1,0:T(8,128)S(1)}, u32[]{:S(2)}, u32[]{:S(2)}) collective-permute-start(f32[18,1]{1,0:T(8,128)S(1)} %get-tuple-element.58), channel_id=1, source_target_pairs={{0,1},{1,2},{2,3},{4,5},{5,6},{6,7},{8,9},{9,10},{10,11},{12,13},{... | collective-permute-start | bytes 224 | tf_op jit(solution)/shard_map/ppermute | solution.py:20
  189.4 1.3 collective-permute-start.15
  190.7 3.1 %collective-permute-done.15 = f32[18,1]{1,0:T(8,128)S(1)} collective-permute-done((f32[18,1]{1,0:T(8,128)S(1)}, f32[18,1]{1,0:T(8,128)S(1)}, u32[]{:S(2)}, u32[]{:S(2)}) %collective-permute-start.15) | collective-permute-done | bytes 104 | tf_op jit(solution)/shard_map/ppermute | solution.py:21
  194.0 3.4 %collective-permute-start.16 = (f32[1,512]{1,0:T(1,128)S(1)}, f32[1,512]{1,0:T(1,128)S(1)}, u32[]{:S(2)}, u32[]{:S(2)}) collective-permute-start(f32[1,512]{1,0:T(1,128)S(1)} %get-tuple-element.62), channel_id=1, source_target_pairs={{0,4},{4,8},{8,12},{12,16},{16,20},{20,24},{24,28},{28,32},{32,36}... | collective-permute-start | bytes 6152 | tf_op jit(solution)/shard_map/ppermute | solution.py:20
  197.4 1.9 collective-permute-start.17
  199.3 2.9 %collective-permute-done.17 = f32[1,512]{1,0:T(1,128)S(1)} collective-permute-done((f32[1,512]{1,0:T(1,128)S(1)}, f32[1,512]{1,0:T(1,128)S(1)}, u32[]{:S(2)}, u32[]{:S(2)}) %collective-permute-start.17) | collective-permute-done | bytes 2080 | tf_op jit(solution)/shard_map/ppermute | solution.py:21
  202.4 2.9 %collective-permute-start.18 = (f32[18,1]{1,0:T(8,128)S(1)}, f32[18,1]{1,0:T(8,128)S(1)}, u32[]{:S(2)}, u32[]{:S(2)}) collective-permute-start(f32[18,1]{1,0:T(8,128)S(1)} %get-tuple-element.56), channel_id=1, source_target_pairs={{0,1},{1,2},{2,3},{4,5},{5,6},{6,7},{8,9},{9,10},{10,11},{12,13},{... | collective-permute-start | bytes 224 | tf_op jit(solution)/shard_map/ppermute | solution.py:20
  205.3 1.3 collective-permute-start.19
  206.6 3.1 %collective-permute-done.19 = f32[18,1]{1,0:T(8,128)S(1)} collective-permute-done((f32[18,1]{1,0:T(8,128)S(1)}, f32[18,1]{1,0:T(8,128)S(1)}, u32[]{:S(2)}, u32[]{:S(2)}) %collective-permute-start.19) | collective-permute-done | bytes 104 | tf_op jit(solution)/shard_map/ppermute | solution.py:21
  209.8 3.4 %collective-permute-start.20 = (f32[1,512]{1,0:T(1,128)S(1)}, f32[1,512]{1,0:T(1,128)S(1)}, u32[]{:S(2)}, u32[]{:S(2)}) collective-permute-start(f32[1,512]{1,0:T(1,128)S(1)} %get-tuple-element.60), channel_id=1, source_target_pairs={{0,4},{4,8},{8,12},{12,16},{16,20},{20,24},{24,28},{28,32},{32,36}... | collective-permute-start | bytes 6152 | tf_op jit(solution)/shard_map/ppermute | solution.py:20
  213.2 1.9 collective-permute-start.21
  215.2 3.0 %collective-permute-done.21 = f32[1,512]{1,0:T(1,128)S(1)} collective-permute-done((f32[1,512]{1,0:T(1,128)S(1)}, f32[1,512]{1,0:T(1,128)S(1)}, u32[]{:S(2)}, u32[]{:S(2)}) %collective-permute-start.21) | collective-permute-done | bytes 2080 | tf_op jit(solution)/shard_map/ppermute | solution.py:21
  218.2 1.6 collective-permute-start.22
  219.8 1.3 collective-permute-start.23
  221.2 3.1 %collective-permute-done.23 = f32[18,1]{1,0:T(8,128)S(1)} collective-permute-done((f32[18,1]{1,0:T(8,128)S(1)}, f32[18,1]{1,0:T(8,128)S(1)}, u32[]{:S(2)}, u32[]{:S(2)}) %collective-permute-start.23) | collective-permute-done | bytes 104 | tf_op jit(solution)/shard_map/ppermute | solution.py:21
  224.4 7.6 %gather_fusion = f32[2048,128]{1,0:T(8,128)} fusion(f32[64,128]{1,0:T(8,128)S(1)} %reshape.121, s32[2048]{0:T(1024)S(1)} %broadcast_clamp_fusion), kind=kCustom, calls=%fused_computation | custom fusion | bytes 2105344 | tf_op jit(solution)/shard_map/gather | solution.py:171
  232.0 18.5 %all-to-all-start.2 = ((f32[64,32,128]{2,1,0:T(8,128)}), f32[64,32,128]{2,1,0:T(8,128)S(1)}, u32[]{:S(2)}, u32[]{:S(2)}) async-start(f32[64,32,128]{2,1,0:T(8,128)} %bitcast.23), calls=%async_computation.2 | async-start | bytes 2097152 | tf_op jit(solution)/shard_map/all_to_all | solution.py:172
  250.6 28.0 %all-to-all-done.2 = f32[64,32,128]{2,1,0:T(8,128)S(1)} async-done(((f32[64,32,128]{2,1,0:T(8,128)}), f32[64,32,128]{2,1,0:T(8,128)S(1)}, u32[]{:S(2)}, u32[]{:S(2)}) %all-to-all-start.2) | async-done | bytes 1048608 | tf_op jit(solution)/shard_map/all_to_all | solution.py:172
  278.5 2.8 gather_fusion.1
  281.3 0.9 reshape.124
  (81 shorter events, 3.1 us)
Async XLA Ops:
  0.6 5.7 %copy-start.7 = (s32[1,1,1024,1]{2,3,1,0:T(1,128)S(1)}, s32[1,1,1024,1]{2,3,1,0:T(1,128)}, u32[]{:S(2)}) copy-start(s32[1,1,1024,1]{2,3,1,0:T(1,128)} %param.10) | copy-start | bytes 12292
  1.7 23.2 %copy-start.1 = (f32[2,256,512]{2,1,0:T(8,128)S(1)}, f32[2,256,512]{2,1,0:T(8,128)}, u32[]{:S(2)}) copy-start(f32[2,256,512]{2,1,0:T(8,128)} %param.8) | copy-start | bytes 3145732
  2.9 22.0 %collective-permute-start = (f32[11,2,512]{2,1,0:T(2,128)S(1)}, f32[11,2,512]{2,1,0:T(2,128)S(1)}, u32[]{:S(2)}, u32[]{:S(2)}) collective-permute-start(f32[11,2,512]{2,1,0:T(2,128)S(1)} %get-tuple-element.30), channel_id=1, source_target_pairs={{0,4},{4,8},{8,12},{12,16},{16,20},{20,24},{24,28},{28,32},{32,36}... | collective-permute-start | bytes 135176 | tf_op jit(solution)/shard_map/ppermute | solution.py:20
  5.6 19.3 %collective-permute-start.1 = (f32[11,2,512]{2,1,0:T(2,128)S(1)}, f32[11,2,512]{2,1,0:T(2,128)S(1)}, u32[]{:S(2)}, u32[]{:S(2)}) collective-permute-start(f32[11,2,512]{2,1,0:T(2,128)S(1)} %get-tuple-element.31), channel_id=1, source_target_pairs={{4,0},{8,4},{12,8},{16,12},{20,16},{24,20},{28,24},{32,28},{36,32}... | collective-permute-start | bytes 135176 | tf_op jit(solution)/shard_map/ppermute | solution.py:21
  30.1 10.8 %collective-permute-start.2 = (f32[11,260,2]{1,2,0:T(2,128)S(1)}, f32[11,260,2]{1,2,0:T(2,128)S(1)}, u32[]{:S(2)}, u32[]{:S(2)}) collective-permute-start(f32[11,260,2]{1,2,0:T(2,128)S(1)} %copy.45), channel_id=1, source_target_pairs={{0,1},{1,2},{2,3},{3,0},{4,5},{5,6},{6,7},{7,4},{8,9},{9,10},{10,1... | collective-permute-start | bytes 68648 | tf_op jit(solution)/shard_map/ppermute | solution.py:20
  31.4 10.1 %collective-permute-start.3 = (f32[11,260,2]{1,2,0:T(2,128)S(1)}, f32[11,260,2]{1,2,0:T(2,128)}, u32[]{:S(2)}, u32[]{:S(2)}) collective-permute-start(f32[11,260,2]{1,2,0:T(2,128)S(1)} %copy.46), channel_id=1, source_target_pairs={{1,0},{2,1},{3,2},{0,3},{5,4},{6,5},{7,6},{4,7},{9,8},{10,9},{11,1... | collective-permute-start | bytes 68648 | tf_op jit(solution)/shard_map/ppermute | solution.py:21
  43.8 3.9 %copy-start.2 = (f32[11,260,2]{2,1,0:T(8,128)S(1)}, f32[11,260,2]{2,1,0:T(8,128)}, u32[]{:S(2)}) copy-start(f32[11,260,2]{2,1,0:T(8,128)} %copy.48) | copy-start | bytes 68644
  45.5 3.1 %copy-start = (f32[8,256,512]{2,1,0:T(8,128)S(1)}, f32[8,256,512]{2,1,0:T(8,128)}, u32[]{:S(2)}) copy-start(f32[8,256,512]{2,1,0:T(8,128)} %param.7) | copy-start | bytes 12582916
  48.9 14.6 %slice-start = ((s8[5947392]{0:T(1024)(128)(4,1)}), s8[4194304]{0:T(1024)(128)(4,1)S(1)}, s32[]{:S(2)}) async-start(s8[5947392]{0:T(1024)(128)(4,1)} %bitcast.54), calls=%async_computation.3 | async-start | bytes 8388608
  48.9 14.6 %slice-start.2 = ((s8[5947392]{0:T(1024)(128)(4,1)}), s8[4194304]{0:T(1024)(128)(4,1)S(1)}, s32[]{:S(2)}) async-start(s8[5947392]{0:T(1024)(128)(4,1)} %bitcast.56), calls=%async_computation.5 | async-start | bytes 8388608
  51.2 12.3 %slice-start.1 = ((s8[5947392]{0:T(1024)(128)(4,1)}), s8[1753088]{0:T(1024)(128)(4,1)S(1)}, s32[]{:S(2)}) async-start(s8[5947392]{0:T(1024)(128)(4,1)} %bitcast.54), calls=%async_computation.4 | async-start | bytes 3506176
  51.2 12.3 %slice-start.3 = ((s8[5947392]{0:T(1024)(128)(4,1)}), s8[1753088]{0:T(1024)(128)(4,1)S(1)}, s32[]{:S(2)}) async-start(s8[5947392]{0:T(1024)(128)(4,1)} %bitcast.56), calls=%async_computation.6 | async-start | bytes 3506176
  63.5 34.5 %copy-start.8 = (s32[1,1,1024,1]{2,3,1,0:T(1,128)S(1)}, s32[1,1,1024,1]{2,3,1,0:T(1,128)}, u32[]{:S(2)}) copy-start(s32[1,1,1024,1]{2,3,1,0:T(1,128)} %param.11) | copy-start | bytes 12292
  87.8 6.6 %copy-start.3 = (f32[8,256,512]{2,1,0:T(8,128)}, f32[8,256,512]{2,1,0:T(8,128)S(1)}, u32[]{:S(2)}) copy-start(f32[8,256,512]{2,1,0:T(8,128)S(1)} %multiply_subtract_fusion) | copy-start | bytes 12582916
  87.8 7.1 %collective-permute-start.4 = (f32[2,1,512]{2,1,0:T(1,128)S(1)}, f32[2,1,512]{2,1,0:T(1,128)S(1)}, u32[]{:S(2)}, u32[]{:S(2)}) collective-permute-start(f32[2,1,512]{2,1,0:T(1,128)S(1)} %get-tuple-element.32), channel_id=1, source_target_pairs={{0,4},{4,8},{8,12},{12,16},{16,20},{20,24},{24,28},{28,32},{32,36}... | collective-permute-start | bytes 12296 | tf_op jit(solution)/shard_map/ppermute | solution.py:20
  89.5 5.7 %collective-permute-start.5 = (f32[2,1,512]{2,1,0:T(1,128)S(1)}, f32[2,1,512]{2,1,0:T(1,128)S(1)}, u32[]{:S(2)}, u32[]{:S(2)}) collective-permute-start(f32[2,1,512]{2,1,0:T(1,128)S(1)} %get-tuple-element.33), channel_id=1, source_target_pairs={{4,0},{8,4},{12,8},{16,12},{20,16},{24,20},{28,24},{32,28},{36,32}... | collective-permute-start | bytes 12296 | tf_op jit(solution)/shard_map/ppermute | solution.py:21
  95.3 22.2 %collective-permute-start.6 = (f32[2,258,1]{2,1,0:T(8,128)S(1)}, f32[2,258,1]{2,1,0:T(8,128)S(1)}, u32[]{:S(2)}, u32[]{:S(2)}) collective-permute-start(f32[2,258,1]{2,1,0:T(8,128)S(1)} %get-tuple-element.36), channel_id=1, source_target_pairs={{0,1},{1,2},{2,3},{3,0},{4,5},{5,6},{6,7},{7,4},{8,9},{9,10},{10,1... | collective-permute-start | bytes 6200 | tf_op jit(solution)/shard_map/ppermute | solution.py:20
  95.5 22.0 %collective-permute-start.7 = (f32[2,258,1]{2,1,0:T(8,128)S(1)}, f32[2,258,1]{2,1,0:T(8,128)S(1)}, u32[]{:S(2)}, u32[]{:S(2)}) collective-permute-start(f32[2,258,1]{2,1,0:T(8,128)S(1)} %get-tuple-element.37), channel_id=1, source_target_pairs={{1,0},{2,1},{3,2},{0,3},{5,4},{6,5},{7,6},{4,7},{9,8},{10,9},{11,1... | collective-permute-start | bytes 6200 | tf_op jit(solution)/shard_map/ppermute | solution.py:21
  103.1 23.7 %all-to-all-start = ((f32[64,1,32]{2,1,0:T(1,128)}), f32[64,1,32]{2,1,0:T(1,128)S(1)}, u32[]{:S(2)}, u32[]{:S(2)}) async-start(f32[64,1,32]{2,1,0:T(1,128)} %bitcast.13), calls=%async_computation | async-start | bytes 65536 | tf_op jit(solution)/shard_map/all_to_all | solution.py:139
  118.1 44.3 %copy-start.4 = (f32[16,512]{1,0:T(8,128)S(1)}, f32[16,512]{1,0:T(8,128)}, u32[]{:S(2)}) copy-start(f32[16,512]{1,0:T(8,128)} %param.13) | copy-start | bytes 98308
  118.1 44.3 %copy-start.5 = (f32[16,512]{1,0:T(8,128)S(1)}, f32[16,512]{1,0:T(8,128)}, u32[]{:S(2)}) copy-start(f32[16,512]{1,0:T(8,128)} %param.12) | copy-start | bytes 98308
  126.8 34.3 %all-to-all-start.1 = ((f32[64,32,128]{2,1,0:T(8,128)}), f32[64,32,128]{2,1,0:T(8,128)S(1)}, u32[]{:S(2)}, u32[]{:S(2)}) async-start(f32[64,32,128]{2,1,0:T(8,128)} %bitcast.16), calls=%async_computation.1 | async-start | bytes 2097152 | tf_op jit(solution)/shard_map/all_to_all | solution.py:132
  162.5 6.3 %collective-permute-start.8 = (f32[3,2,512]{2,1,0:T(2,128)S(1)}, f32[3,2,512]{2,1,0:T(2,128)S(1)}, u32[]{:S(2)}, u32[]{:S(2)}) collective-permute-start(f32[3,2,512]{2,1,0:T(2,128)S(1)} %get-tuple-element.52), channel_id=1, source_target_pairs={{0,4},{4,8},{8,12},{12,16},{16,20},{20,24},{24,28},{28,32},{32,36}... | collective-permute-start | bytes 36872 | tf_op jit(solution)/shard_map/ppermute | solution.py:20
  166.8 5.0 %collective-permute-start.9 = (f32[3,2,512]{2,1,0:T(2,128)S(1)}, f32[3,2,512]{2,1,0:T(2,128)S(1)}, u32[]{:S(2)}, u32[]{:S(2)}) collective-permute-start(f32[3,2,512]{2,1,0:T(2,128)S(1)} %get-tuple-element.53), channel_id=1, source_target_pairs={{4,0},{8,4},{12,8},{16,12},{20,16},{24,20},{28,24},{32,28},{36,32}... | collective-permute-start | bytes 36872 | tf_op jit(solution)/shard_map/ppermute | solution.py:21
  171.9 2.6 collective-permute-start.10
  173.2 4.7 %collective-permute-start.11 = (f32[3,20,2]{2,1,0:T(8,128)S(1)}, f32[3,20,2]{2,1,0:T(8,128)S(1)}, u32[]{:S(2)}, u32[]{:S(2)}) collective-permute-start(f32[3,20,2]{2,1,0:T(8,128)S(1)} %get-tuple-element.51), channel_id=1, source_target_pairs={{1,0},{2,1},{3,2},{5,4},{6,5},{7,6},{9,8},{10,9},{11,10},{13,12},{... | collective-permute-start | bytes 1448 | tf_op jit(solution)/shard_map/ppermute | solution.py:21
  178.3 5.2 %collective-permute-start.12 = (f32[1,512]{1,0:T(1,128)S(1)}, f32[1,512]{1,0:T(1,128)S(1)}, u32[]{:S(2)}, u32[]{:S(2)}) collective-permute-start(f32[1,512]{1,0:T(1,128)S(1)} %get-tuple-element.64), channel_id=1, source_target_pairs={{0,4},{4,8},{8,12},{12,16},{16,20},{20,24},{24,28},{28,32},{32,36}... | collective-permute-start | bytes 6152 | tf_op jit(solution)/shard_map/ppermute | solution.py:20
  181.4 4.9 %collective-permute-start.13 = (f32[1,512]{1,0:T(1,128)S(1)}, f32[1,512]{1,0:T(1,128)S(1)}, u32[]{:S(2)}, u32[]{:S(2)}) collective-permute-start(f32[1,512]{1,0:T(1,128)S(1)} %get-tuple-element.65), channel_id=1, source_target_pairs={{4,0},{8,4},{12,8},{16,12},{20,16},{24,20},{28,24},{32,28},{36,32}... | collective-permute-start | bytes 6152 | tf_op jit(solution)/shard_map/ppermute | solution.py:21
  186.4 4.4 %collective-permute-start.14 = (f32[18,1]{1,0:T(8,128)S(1)}, f32[18,1]{1,0:T(8,128)S(1)}, u32[]{:S(2)}, u32[]{:S(2)}) collective-permute-start(f32[18,1]{1,0:T(8,128)S(1)} %get-tuple-element.58), channel_id=1, source_target_pairs={{0,1},{1,2},{2,3},{4,5},{5,6},{6,7},{8,9},{9,10},{10,11},{12,13},{... | collective-permute-start | bytes 224 | tf_op jit(solution)/shard_map/ppermute | solution.py:20
  189.4 4.4 %collective-permute-start.15 = (f32[18,1]{1,0:T(8,128)S(1)}, f32[18,1]{1,0:T(8,128)S(1)}, u32[]{:S(2)}, u32[]{:S(2)}) collective-permute-start(f32[18,1]{1,0:T(8,128)S(1)} %get-tuple-element.59), channel_id=1, source_target_pairs={{1,0},{2,1},{3,2},{5,4},{6,5},{7,6},{9,8},{10,9},{11,10},{13,12},{... | collective-permute-start | bytes 224 | tf_op jit(solution)/shard_map/ppermute | solution.py:21
  194.0 5.3 %collective-permute-start.16 = (f32[1,512]{1,0:T(1,128)S(1)}, f32[1,512]{1,0:T(1,128)S(1)}, u32[]{:S(2)}, u32[]{:S(2)}) collective-permute-start(f32[1,512]{1,0:T(1,128)S(1)} %get-tuple-element.62), channel_id=1, source_target_pairs={{0,4},{4,8},{8,12},{12,16},{16,20},{20,24},{24,28},{28,32},{32,36}... | collective-permute-start | bytes 6152 | tf_op jit(solution)/shard_map/ppermute | solution.py:20
  197.4 4.9 %collective-permute-start.17 = (f32[1,512]{1,0:T(1,128)S(1)}, f32[1,512]{1,0:T(1,128)S(1)}, u32[]{:S(2)}, u32[]{:S(2)}) collective-permute-start(f32[1,512]{1,0:T(1,128)S(1)} %get-tuple-element.63), channel_id=1, source_target_pairs={{4,0},{8,4},{12,8},{16,12},{20,16},{24,20},{28,24},{32,28},{36,32}... | collective-permute-start | bytes 6152 | tf_op jit(solution)/shard_map/ppermute | solution.py:21
  202.4 4.2 %collective-permute-start.18 = (f32[18,1]{1,0:T(8,128)S(1)}, f32[18,1]{1,0:T(8,128)S(1)}, u32[]{:S(2)}, u32[]{:S(2)}) collective-permute-start(f32[18,1]{1,0:T(8,128)S(1)} %get-tuple-element.56), channel_id=1, source_target_pairs={{0,1},{1,2},{2,3},{4,5},{5,6},{6,7},{8,9},{9,10},{10,11},{12,13},{... | collective-permute-start | bytes 224 | tf_op jit(solution)/shard_map/ppermute | solution.py:20
  205.3 4.4 %collective-permute-start.19 = (f32[18,1]{1,0:T(8,128)S(1)}, f32[18,1]{1,0:T(8,128)S(1)}, u32[]{:S(2)}, u32[]{:S(2)}) collective-permute-start(f32[18,1]{1,0:T(8,128)S(1)} %get-tuple-element.57), channel_id=1, source_target_pairs={{1,0},{2,1},{3,2},{5,4},{6,5},{7,6},{9,8},{10,9},{11,10},{13,12},{... | collective-permute-start | bytes 224 | tf_op jit(solution)/shard_map/ppermute | solution.py:21
  209.8 5.3 %collective-permute-start.20 = (f32[1,512]{1,0:T(1,128)S(1)}, f32[1,512]{1,0:T(1,128)S(1)}, u32[]{:S(2)}, u32[]{:S(2)}) collective-permute-start(f32[1,512]{1,0:T(1,128)S(1)} %get-tuple-element.60), channel_id=1, source_target_pairs={{0,4},{4,8},{8,12},{12,16},{16,20},{20,24},{24,28},{28,32},{32,36}... | collective-permute-start | bytes 6152 | tf_op jit(solution)/shard_map/ppermute | solution.py:20
  213.2 4.9 %collective-permute-start.21 = (f32[1,512]{1,0:T(1,128)S(1)}, f32[1,512]{1,0:T(1,128)S(1)}, u32[]{:S(2)}, u32[]{:S(2)}) collective-permute-start(f32[1,512]{1,0:T(1,128)S(1)} %get-tuple-element.61), channel_id=1, source_target_pairs={{4,0},{8,4},{12,8},{16,12},{20,16},{24,20},{28,24},{32,28},{36,32}... | collective-permute-start | bytes 6152 | tf_op jit(solution)/shard_map/ppermute | solution.py:21
  218.2 2.9 %collective-permute-start.22 = (f32[18,1]{1,0:T(8,128)S(1)}, f32[18,1]{1,0:T(8,128)S(1)}, u32[]{:S(2)}, u32[]{:S(2)}) collective-permute-start(f32[18,1]{1,0:T(8,128)S(1)} %get-tuple-element.54), channel_id=1, source_target_pairs={{0,1},{1,2},{2,3},{4,5},{5,6},{6,7},{8,9},{9,10},{10,11},{12,13},{... | collective-permute-start | bytes 224 | tf_op jit(solution)/shard_map/ppermute | solution.py:20
  219.8 4.4 %collective-permute-start.23 = (f32[18,1]{1,0:T(8,128)S(1)}, f32[18,1]{1,0:T(8,128)S(1)}, u32[]{:S(2)}, u32[]{:S(2)}) collective-permute-start(f32[18,1]{1,0:T(8,128)S(1)} %get-tuple-element.55), channel_id=1, source_target_pairs={{1,0},{2,1},{3,2},{5,4},{6,5},{7,6},{9,8},{10,9},{11,10},{13,12},{... | collective-permute-start | bytes 224 | tf_op jit(solution)/shard_map/ppermute | solution.py:21
  224.4 7.6 %copy-start.6 = (f32[16,512]{1,0:T(8,128)}, f32[16,512]{1,0:T(8,128)S(1)}, u32[]{:S(2)}) copy-start(f32[16,512]{1,0:T(8,128)S(1)} %fusion.21) | copy-start | bytes 98308
  232.0 46.5 %all-to-all-start.2 = ((f32[64,32,128]{2,1,0:T(8,128)}), f32[64,32,128]{2,1,0:T(8,128)S(1)}, u32[]{:S(2)}, u32[]{:S(2)}) async-start(f32[64,32,128]{2,1,0:T(8,128)} %bitcast.23), calls=%async_computation.2 | async-start | bytes 2097152 | tf_op jit(solution)/shard_map/all_to_all | solution.py:172
where the time goes:
time: 283 us; the launch traced here: 282 us
  starting transfers between devices  90.5 us (32%)
  waiting for transfers between devices  83.8 us (30%)
  other arithmetic  74.8 us (26%)
  local copies, waits for them, and re-layouts  30.4 us (11%)
    ppermute x12, starting transfers between devices, with_halo(): before = lax.ppermute(last, axis, up)  28.2 us
    all_to_all x1, waiting for transfers between devices, on_device(): lax.all_to_all(picked.reshape(sections, capacity, 128), 'sec', split_axis...  28 us
    all_to_all x1, waiting for transfers between devices, on_device(): lax.all_to_all(send_blocks.reshape(sections, capacity, 128), 'sec', split...  26.7 us
    ppermute x12, waiting for transfers between devices, with_halo(): after = lax.ppermute(leading, axis, down)  24.8 us
    sub x1, other arithmetic, advance(): window(field, 0, 0)  24.2 us
    concatenate x5, other arithmetic, with_halo(): shard = jnp.concatenate([before, shard, after], axis=dim)  23.6 us
    ppermute x12, starting transfers between devices, with_halo(): after = lax.ppermute(leading, axis, down)  23.2 us
    all_to_all x1, starting transfers between devices, on_device(): lax.all_to_all(picked.reshape(sections, capacity, 128), 'sec', split_axis...  18.5 us
  transfers between devices with their start and end apart: 27, of which 13 were waited for; matrix products, arithmetic and copies ran while one was open for 14% of the time, Pallas kernels for 0%

commit v1 on v0

v1 whole, which is shorter than its diff:
```python
import jax
import jax.numpy as jnp
from jax import lax
from jax.experimental import pallas as pl
from jax.experimental.pallas import tpu as pltpu
from jax.sharding import PartitionSpec as P

ITERS = 4
CORES = 2
TOP = 16
PAD = 40
GROUPS = 8
MESH = pl.DeviceIdType.MESH


def minmod(a, b):
    return jnp.maximum(jnp.minimum(a, b), jnp.minimum(jnp.maximum(a, b), 0.0))


def lane_next(tiles, lane):
    rolled = [pltpu.roll(t, 127, 1) for t in tiles]
    n = len(tiles)
    return [jnp.where(lane == 127, rolled[(j + 1) % n], rolled[j]) for j in range(n)]


def lane_prev(tiles, lane):
    rolled = [pltpu.roll(t, 1, 1) for t in tiles]
    return [jnp.where(lane == 0, rolled[j - 1], rolled[j]) for j in range(len(tiles))]


def kernel(
    dims,
    state,
    velocity,
    limiter,
    sigma,
    prior,
    row_target,
    target,
    out_state,
    out_phi,
    out_foot,
    grid,
    flags,
    fresh,
    face_x,
    face_y,
    packs,
    edges,
    corners,
    packs_o,
    edges_o,
    shell,
    weights,
    dense_sib,
    dense_own,
    got_sib,
    got_x,
    z_part,
    got_z,
    table,
    foot,
    load_sem,
    out_sem,
    send_sem,
    recv_sem,
):
    zs, xs, secs, blks, nq, cx, cy, lat, lon = dims
    nj = cy // 128
    sb = lat * lon // 128
    me = lax.axis_index("sec")
    col = lax.axis_index("blk")
    core = lax.rem(me, CORES)
    at_x = lax.rem(lax.div(me, CORES), xs)
    at_z = lax.div(me, CORES * xs)

    def sec_of(z, x, c):
        return (z * xs + x) * CORES + c

    up, down = lax.rem(me + secs - 1, secs), lax.rem(me + 1, secs)
    left, right = lax.rem(col + blks - 1, blks), lax.rem(col + 1, blks)
    sibling = (me + 1 - 2 * core, col)
    x_peer = {d: (sec_of(at_z, lax.rem(at_x + d, xs), core), col) for d in range(1, xs)}
    z_peer = {d: (sec_of(lax.rem(at_z + d, zs), at_x, core), col) for d in range(1, zs)}
    compass = {
        (-1, 0): (up, col),
        (1, 0): (down, col),
        (0, -1): (me, left),
        (0, 1): (me, right),
        (-1, -1): (up, left),
        (-1, 1): (up, right),
        (1, -1): (down, left),
        (1, 1): (down, right),
    }

    used = [0]
    sent = []

    def send(src, dst, device):
        n = used[0]
        used[0] += 1
        copy = pltpu.make_async_remote_copy(
            src_ref=src,
            dst_ref=dst,
            send_sem=send_sem.at[n],
            recv_sem=recv_sem.at[n],
            device_id=device,
            device_id_type=MESH,
        )
        copy.start()
        sent.append(copy)
        return copy

    loads = {}

    def load(name, src, dst):
        copy = pltpu.make_async_copy(src, dst, load_sem.at[len(loads)])
        copy.start()
        loads[name] = copy

    mid = slice(TOP, TOP + cx)
    for j in range(nj):
        lanes = slice(128 * j, 128 * j + 128)
        load(("f", j), state.at[nq - 2 : nq, :, lanes], grid.at[nq - 2 : nq, j, mid, :])
        load(("v", j), velocity.at[:, :, lanes], grid.at[nq : nq + 2, j, mid, :])
        load(("l", j), limiter.at[:, lanes], flags.at[j])
    load("sigma", sigma, shell.at[0, 8 : 8 + lat, 128 : 128 + lon])
    load("prior", prior, shell.at[1, 8 : 8 + lat, 128 : 128 + lon])
    for j in range(nj):
        lanes = slice(128 * j, 128 * j + 128)
        load(("o", j), state.at[: nq - 2, :, lanes], grid.at[: nq - 2, j, mid, :])

    barrier = pltpu.get_barrier_semaphore()
    partners = [*compass.values(), *x_peer.values(), *z_peer.values(), sibling]
    for device in partners:
        pl.semaphore_signal(barrier, inc=1, device_id=device, device_id_type=MESH)
    pl.semaphore_wait(barrier, len(partners))

    lane = lax.broadcasted_iota(jnp.int32, (8, 128), 1)
    sub = lax.broadcasted_iota(jnp.int32, (8, 128), 0)

    for j in range(nj):
        for name in ("f", "v", "l"):
            loads[(name, j)].wait()
    for j in range(nj):
        grid[nq + 2, j, mid, :] = 0.5 * flags[j].astype(jnp.float32)
    first = nq - 2
    fields = slice(first, first + 5)
    top, bottom = slice(TOP, TOP + 8), slice(TOP + cx - 8, TOP + cx)
    above, below = slice(TOP - 8, TOP), slice(TOP + cx, TOP + cx + 8)
    halo = []
    halo.append(send(grid.at[fields, 0:nj, bottom, :], grid.at[fields, 0:nj, above, :], (down, col)))
    halo.append(send(grid.at[fields, 0:nj, top, :], grid.at[fields, 0:nj, below, :], (up, col)))

    rows = cx // GROUPS
    wide = lax.broadcasted_iota(jnp.int32, (rows, 128), 1)

    def pack(base, count, width):
        at_left = jnp.zeros((rows, 128), jnp.float32)
        at_right = jnp.zeros((rows, 128), jnp.float32)
        for g in range(GROUPS):
            here = slice(TOP + g * rows, TOP + (g + 1) * rows)
            for a in range(count):
                at = 16 * g + width * a
                mask = (wide >= at) & (wide < at + width)
                at_left = jnp.where(mask, pltpu.roll(grid[base + a, 0, here, :], at, 1), at_left)
                moved = pltpu.roll(grid[base + a, nj - 1, here, :], (at + width) % 128, 1)
                at_right = jnp.where(mask, moved, at_right)
        return at_left, at_right

    def unpack(base, count, width, from_left, from_right, take, put, size, group):
        side = lax.broadcasted_iota(jnp.int32, (size, 128), 1) < 64
        for a in range(count):
            at = 16 * group + width * a
            r = pltpu.roll(from_right[take, :], (128 - at) % 128, 1)
            l = pltpu.roll(from_left[take, :], (256 - width - at) % 128, 1)
            grid[base + a, nj, put, :] = jnp.where(side, r, l)

    to_left, to_right = pack(first, 5, 3)
    packs[0] = to_left
    packs[1] = to_right
    halo.append(send(packs.at[1], edges.at[0], (me, right)))
    halo.append(send(packs.at[0], edges.at[1], (me, left)))
    halo.append(send(packs.at[1, rows - 8 : rows, :], corners.at[0], (down, right)))
    halo.append(send(packs.at[0, rows - 8 : rows, :], corners.at[1], (down, left)))
    halo.append(send(packs.at[1, 0:8, :], corners.at[2], (up, right)))
    halo.append(send(packs.at[0, 0:8, :], corners.at[3], (up, left)))

    row_src = {0: slice(8, 8 + lat), 1: slice(lat, lat + 8), -1: slice(8, 16)}
    row_dst = {0: slice(8, 8 + lat), 1: slice(0, 8), -1: slice(8 + lat, 16 + lat)}
    lane_src = {0: slice(128, 128 + lon), 1: slice(lon, lon + 128), -1: slice(128, 256)}
    lane_dst = {0: slice(128, 128 + lon), 1: slice(0, 128), -1: slice(128 + lon, 256 + lon)}

    def shell_halo(which):
        return [
            send(
                shell.at[which, row_src[dr], lane_src[dc]],
                shell.at[which, row_dst[dr], lane_dst[dc]],
                device,
            )
            for (dr, dc), device in compass.items()
        ]

    loads["sigma"].wait()
    loads["prior"].wait()
    shell_copies = shell_halo(slice(0, 2))

    for j in range(nj):
        loads[("o", j)].wait()
    others = slice(0, nq - 2)
    halo_o = [
        send(grid.at[others, 0:nj, bottom, :], grid.at[others, 0:nj, above, :], (down, col)),
        send(grid.at[others, 0:nj, top, :], grid.at[others, 0:nj, below, :], (up, col)),
    ]
    to_left, to_right = pack(0, nq - 2, 2)
    packs_o[0] = to_left
    packs_o[1] = to_right
    halo_o.append(send(packs_o.at[1], edges_o.at[0], (me, right)))
    halo_o.append(send(packs_o.at[0], edges_o.at[1], (me, left)))

    for copy in halo:
        copy.wait_recv()
    for g in range(GROUPS):
        here = slice(TOP + g * rows, TOP + (g + 1) * rows)
        unpack(first, 5, 3, edges.at[0], edges.at[1], slice(0, rows), here, rows, g)
    unpack(first, 5, 3, corners.at[0], corners.at[1], slice(0, 8), above, 8, GROUPS - 1)
    unpack(first, 5, 3, corners.at[2], corners.at[3], slice(0, 8), below, 8, 0)

    def tile(ref, *at):
        return ref[at]

    def faces(k, carry):
        b = pl.multiple_of(8 * k, 8)
        speed_y = [grid[nq + 1, j, pl.ds(b, 8), :] for j in range(nj + 1)]
        for j, (here, after) in enumerate(zip(speed_y, lane_next(speed_y, lane))):
            face_y[j, pl.ds(b, 8), :] = 0.2 * (here + after)
            face_x[j, pl.ds(b, 8), :] = 0.2 * (
                grid[nq, j, pl.ds(b, 8), :] + grid[nq, j, pl.ds(b + 1, 8), :]
            )
        return carry

    lax.fori_loop(1, TOP // 8 + cx // 8 + 1, faces, 0)

    def advect(q, tiles_x, last):
        def slopes(k):
            b = pl.multiple_of(8 * k, 8)
            lefts, rights = [], []
            for j in range(tiles_x):
                here = grid[q, j, pl.ds(b, 8), :]
                lower = here - grid[q, j, pl.ds(b - 1, 8), :]
                upper = grid[q, j, pl.ds(b + 1, 8), :] - here
                half = minmod(lower, upper) * grid[nq + 2, j, pl.ds(b, 8), :]
                lefts.append(here + half)
                rights.append(here - half)
            return tuple(lefts), tuple(pltpu.roll(r, 7, 0) for r in rights)

        def step(k, carry):
            lefts, rights, flux_before = carry
            lefts_k, rights_k = slopes(k)
            b = pl.multiple_of(8 * (k - 1), 8)
            here = [grid[q, j, pl.ds(b, 8), :] for j in range(nj + 1)]
            diff = [after - h for h, after in zip(here, lane_next(here, lane))]
            lim = [grid[nq + 2, j, pl.ds(b, 8), :] for j in range(nj + 1)]
            half = [
                minmod(lower, upper) * w
                for lower, upper, w in zip(lane_prev(diff, lane), diff, lim)
            ]
            after = lane_next([h - s for h, s in zip(here, half)], lane)
            flux_y = []
            for j in range(nj + 1):
                speed = face_y[j, pl.ds(b, 8), :]
                flux_y.append(speed * jnp.where(speed > 0.0, here[j] + half[j], after[j]))
            before_y = lane_prev(flux_y, lane)
            flux_rolled = []
            for j in range(tiles_x):
                speed = face_x[j, pl.ds(b, 8), :]
                follow = jnp.where(sub == 7, rights_k[j], rights[j])
                flux = speed * jnp.where(speed > 0.0, lefts[j], follow)
                rolled = pltpu.roll(flux, 1, 0)
                flux_rolled.append(rolled)
                change = (flux - jnp.where(sub == 0, flux_before[j], rolled)) + (
                    flux_y[j] - before_y[j]
                )
                fresh[q, j, pl.ds(b, 8), :] = here[j] - change
            return lefts_k, rights_k, tuple(flux_rolled)

        zero = tuple(jnp.zeros((8, 128), jnp.float32) for _ in range(tiles_x))
        lefts, rights = slopes(1)
        lax.fori_loop(2, last + 1, step, (lefts, rights, zero))

    end = TOP // 8 + cx // 8 + 1
    advect(nq - 2, nj + 1, end)
    advect(nq - 1, nj + 1, end)

    writes = []

    def write(src, dst):
        copy = pltpu.make_async_copy(src, dst, out_sem.at[len(writes)])
        copy.start()
        writes.append(copy)

    for j in range(nj):
        lanes = slice(128 * j, 128 * j + 128)
        write(fresh.at[nq - 2 : nq, j, mid, :], out_state.at[nq - 2 : nq, :, lanes])

    chunk = 16
    lane_c = lax.broadcasted_iota(jnp.int32, (chunk, 128), 1)

    def curl(k, carry):
        b = pl.multiple_of(TOP + chunk * k, 8)
        field_x = [fresh[nq - 2, j, pl.ds(b, chunk), :] for j in range(nj + 1)]
        after = lane_next(field_x, lane_c)
        before = lane_prev(field_x, lane_c)
        for j in range(nj):
            current = 0.5 * (
                fresh[nq - 1, j, pl.ds(b + 1, chunk), :] - fresh[nq - 1, j, pl.ds(b - 1, chunk), :]
            ) - 0.5 * (after[j] - before[j])
            high = current.astype(jnp.bfloat16)
            low = (current - high.astype(jnp.float32)).astype(jnp.bfloat16)
            r = pl.multiple_of(j * cx + chunk * k, chunk)
            weights[pl.ds(r, chunk), 0:128] = high
            weights[pl.ds(r, chunk), 128:256] = low
        return carry

    lax.fori_loop(0, cx // chunk, curl, 0)

    per_x = zs * sb
    size = min(256, per_x)

    def sums(base, store):
        def one(i, carry):
            at = pl.multiple_of(i * size, size)
            ids = lax.broadcasted_iota(jnp.int32, (size, nj * cx), 0) + (base + at)
            chosen = jnp.where(ids == row_target[...], 1.0, 0.0).astype(jnp.bfloat16)
            both = jnp.dot(chosen, weights[...], preferred_element_type=jnp.float32)
            store[pl.ds(at, size), :] = both[:, :128] + both[:, 128:]
            return carry

        lax.fori_loop(0, per_x // size, one, 0)

    order = sorted(range(1, xs), key=lambda d: -min(d, xs - d)) + [0]
    sib_copies, x_copies = {}, {}

    def for_sibling(d):
        base = ((1 - core) * xs + lax.rem(at_x + d, xs)) * per_x
        sums(base, dense_sib.at[d])
        sib_copies[d] = send(dense_sib.at[d], got_sib.at[d], sibling)

    def for_own(d):
        base = (core * xs + lax.rem(at_x + d, xs)) * per_x
        sums(base, dense_own.at[d])
        sib_copies[d].wait_recv()
        dense_own[d] = dense_own[d] + got_sib[d]
        if d:
            x_copies[d] = send(dense_own.at[d], got_x.at[d - 1], x_peer[d])

    for_sibling(order[0])
    for i, d in enumerate(order):
        if i + 1 < len(order):
            for_sibling(order[i + 1])
        for_own(d)

    for copy in halo_o:
        copy.wait_recv()
    for g in range(GROUPS):
        here = slice(TOP + g * rows, TOP + (g + 1) * rows)
        unpack(0, nq - 2, 2, edges_o.at[0], edges_o.at[1], slice(0, rows), here, rows, g)

    def other(q, carry):
        advect(q, nj, end - 1)
        return carry

    lax.fori_loop(0, nq - 2, other, 0)
    for j in range(nj):
        lanes = slice(128 * j, 128 * j + 128)
        write(fresh.at[0 : nq - 2, j, mid, :], out_state.at[0 : nq - 2, :, lanes])

    for copy in x_copies.values():
        copy.wait_recv()
    total = dense_own[0]
    for d in range(1, xs):
        total = total + got_x[d - 1]
    z_part[...] = total
    z_copies = []
    for d in range(1, zs):
        at = pl.multiple_of(lax.rem(at_z + d, zs) * sb, sb)
        z_copies.append(send(z_part.at[pl.ds(at, sb), :], got_z.at[d - 1], z_peer[d]))
    source = z_part[pl.ds(pl.multiple_of(at_z * sb, sb), sb), :]
    for d in range(1, zs):
        z_copies[d - 1].wait_recv()
        source = source + got_z[d - 1]
    for c in range(lon // 128):
        at = 128 + 128 * c
        shell[2, 8 : 8 + lat, at : at + 128] = source[c * lat : (c + 1) * lat, :]
    source_copies = shell_halo(slice(2, 3))

    for copy in shell_copies:
        copy.wait_recv()
    shape = (lat + 16, lon + 256)
    lat_at = lax.broadcasted_iota(jnp.int32, shape, 0) + (me * lat - 8)
    lon_at = lax.broadcasted_iota(jnp.int32, shape, 1) + (col * lon - 128)
    inside = (lat_at >= 0) & (lat_at < secs * lat) & (lon_at >= 0) & (lon_at < blks * lon)
    sig = jnp.where(inside, shell[0], 0.0)
    phi = jnp.where(inside, shell[1], 0.0)

    def around(a):
        return (
            pltpu.roll(a, 1, 0),
            pltpu.roll(a, lat + 15, 0),
            pltpu.roll(a, 1, 1),
            pltpu.roll(a, lon + 255, 1),
        )

    ways = [0.5 * (sig + other_sig) for other_sig in around(sig)]
    inverse = 1.0 / (ways[0] + ways[1] + ways[2] + ways[3] + 1.0)
    for copy in source_copies:
        copy.wait_recv()
    src = shell[2]
    for _ in range(ITERS):
        n, s, w, e = around(phi)
        total = ways[0] * n + ways[1] * s + ways[2] * w + ways[3] * e + src
        phi = jnp.where(inside, total * inverse, 0.0)
    phi = phi[8 : 8 + lat, 128 : 128 + lon]
    out_phi[...] = phi

    def piece(z, x, c):
        return table.at[pl.ds(pl.multiple_of(((c * xs + x) * zs + z) * sb, sb), sb), :]

    mine = ((core * xs + at_x) * zs + at_z) * sb
    for c in range(lon // 128):
        at = pl.multiple_of(mine + c * lat, lat)
        table[pl.ds(at, lat), :] = phi[:, c * 128 : (c + 1) * 128]

    from_z, from_x, from_sib = {}, {}, []
    own = piece(at_z, at_x, core)
    nearest = sorted(range(1, zs), key=lambda d: min(d, zs - d))
    for d in nearest:
        from_z[d] = send(own, own, z_peer[d])
    for dz in [0] + nearest:
        if dz:
            from_z[dz].wait_recv()
        z = lax.rem(at_z + zs - dz, zs)
        part = piece(z, at_x, core)
        for dx in range(1, xs):
            from_x[dz, dx] = send(part, part, x_peer[dx])
        from_sib.append(send(part, part, sibling))
    for dz in [0] + nearest:
        for dx in range(1, xs):
            from_x[dz, dx].wait_recv()
            z = lax.rem(at_z + zs - dz, zs)
            part = piece(z, lax.rem(at_x + xs - dx, xs), core)
            from_sib.append(send(part, part, sibling))
    for copy in from_sib:
        copy.wait_recv()

    def look_up(k, carry):
        b = pl.multiple_of(8 * k, 8)
        for r in range(8):
            for j in range(nj):
                at = target[(b + r) * nj + j]
                foot[j, pl.ds(b + r, 1), :] = table[pl.ds(at, 1), :]
        return carry

    lax.fori_loop(0, cx // 8, look_up, 0)
    for j in range(nj):
        write(foot.at[j], out_foot.at[:, 128 * j : 128 * j + 128])
    for copy in sent:
        copy.wait_send()
    for copy in writes:
        copy.wait()


def on_device(
    state, velocity, limiter, footpoint_owner, footpoint_slot, conductance, potential_prior
):
    secs, blks = lax.axis_size("sec"), lax.axis_size("blk")
    xs = 4 if secs % 8 == 0 and secs >= 32 else 2
    zs = secs // (CORES * xs)
    nq, cx, cy = state.shape
    lat, lon = conductance.shape
    nj = cy // 128
    sb = lat * lon // 128
    blocks = nj * cx
    owner = footpoint_owner.reshape(blocks)
    slot = footpoint_slot.reshape(blocks)
    per_row = lon // 128
    slot = (slot % per_row) * lat + slot // per_row
    core, x, z = owner % CORES, owner // CORES % xs, owner // (CORES * xs)
    target = ((core * xs + x) * zs + z) * sb + slot
    row_target = target.reshape(cx, nj).T.reshape(1, blocks)

    dims = (zs, xs, secs, blks, nq, cx, cy, lat, lon)
    f32 = jnp.float32
    rows = cx // GROUPS
    per_x = zs * sb
    messages = 12 + 8 + 8 + xs + (xs - 1) + (zs - 1) + (zs - 1) + zs * (xs - 1) + zs * xs
    any_space = pl.BlockSpec(memory_space=pl.ANY)
    vmem = pl.BlockSpec(memory_space=pltpu.VMEM)
    smem = pl.BlockSpec(memory_space=pltpu.SMEM)

    def body(*refs):
        kernel(dims, *refs)

    return pl.pallas_call(
        body,
        out_shape=(
            jax.ShapeDtypeStruct(state.shape, f32),
            jax.ShapeDtypeStruct(conductance.shape, f32),
            jax.ShapeDtypeStruct((cx, cy), f32),
        ),
        in_specs=[any_space] * 5 + [vmem, smem],
        out_specs=(any_space, vmem, any_space),
        scratch_shapes=[
            pltpu.VMEM((nq + 3, nj + 1, cx + PAD, 128), f32),
            pltpu.VMEM((nj, cx, 128), jnp.int32),
            pltpu.VMEM((nq, nj + 1, cx + PAD, 128), f32),
            pltpu.VMEM((nj + 1, cx + PAD, 128), f32),
            pltpu.VMEM((nj + 1, cx + PAD, 128), f32),
            pltpu.VMEM((2, rows, 128), f32),
            pltpu.VMEM((2, rows, 128), f32),
            pltpu.VMEM((4, 8, 128), f32),
            pltpu.VMEM((2, rows, 128), f32),
            pltpu.VMEM((2, rows, 128), f32),
            pltpu.VMEM((3, lat + 16, lon + 256), f32),
            pltpu.VMEM((blocks, 256), jnp.bfloat16),
            pltpu.VMEM((xs, per_x, 128), f32),
            pltpu.VMEM((xs, per_x, 128), f32),
            pltpu.VMEM((xs, per_x, 128), f32),
            pltpu.VMEM((xs - 1, per_x, 128), f32),
            pltpu.VMEM((per_x, 128), f32),
            pltpu.VMEM((zs - 1, sb, 128), f32),
            pltpu.VMEM((secs * sb, 128), f32),
            pltpu.VMEM((nj, cx, 128), f32),
            pltpu.SemaphoreType.DMA((4 * nj + 2,)),
            pltpu.SemaphoreType.DMA((3 * nj,)),
            pltpu.SemaphoreType.DMA((messages,)),
            pltpu.SemaphoreType.DMA((messages,)),
        ],
        compiler_params=pltpu.CompilerParams(
            collective_id=0, has_side_effects=True, vmem_limit_bytes=56 * 1024 * 1024
        ),
    )(state, velocity, limiter, conductance, potential_prior, row_target, target)


def solution(mesh):
    in_specs = (
        P(None, "sec", "blk"),
        P(None, "sec", "blk"),
        P("sec", "blk"),
        P("sec", "blk", None, None),
        P("sec", "blk", None, None),
        P("sec", "blk"),
        P("sec", "blk"),
    )
    out_specs = (P(None, "sec", "blk"), P("sec", "blk"), P("sec", "blk"))
    return jax.shard_map(
        on_device, mesh=mesh, in_specs=in_specs, out_specs=out_specs, check_vma=False
    )
```

time: 283 us -> 154 us (0.54)
  Pallas kernels: 0 us -> 141 us
  starting transfers between devices: 90.5 us -> 0 us
  waiting for transfers between devices: 83.8 us -> 0 us
  other arithmetic: 74.8 us -> 4.37 us
  local copies, waits for them, and re-layouts: 30.4 us -> 7.57 us
    pallas_call x0 -> x1, Pallas kernels: none -> 141 us  [on_device(): pl.pallas_call(body, out_shape=(jax.ShapeDtypeStruct(state.shape, f32), j...]
    all_to_all x3 -> x0, waiting for transfers between devices: 58.6 us -> none  [the longest x1 28 us: on_device(): lax.all_to_all(picked.reshape(sections, capacity, 128), 'sec', split_axis...]
    ppermute x24 -> x0, starting transfers between devices: 51.4 us -> none  [the longest x12 28.2 us: with_halo(): before = lax.ppermute(last, axis, up)]
    all_to_all x3 -> x0, starting transfers between devices: 39.2 us -> none  [the longest x1 18.5 us: on_device(): lax.all_to_all(picked.reshape(sections, capacity, 128), 'sec', split_axis...]
    ppermute x24 -> x0, waiting for transfers between devices: 25.2 us -> none  [the longest x12 24.8 us: with_halo(): after = lax.ppermute(leading, axis, down)]
    sub x2 -> x0, other arithmetic: 24.8 us -> none  [the longest x1 24.2 us: advance(): window(field, 0, 0)]
    concatenate x5 -> x0, other arithmetic: 23.6 us -> none  [with_halo(): shard = jnp.concatenate([before, shard, after], axis=dim)]
    another operation x3 -> x0, other arithmetic: 18.2 us -> none
  transfers between devices with their start and end apart: 27 -> 0, of which waited for: 13 -> 0; matrix products, arithmetic and copies ran while one was open for 14% -> 0% of each run, Pallas kernels for 0% -> 0%
where the time goes in v1:
time: 154 us; the launch traced here: 153 us
  Pallas kernels  141 us (92%)
  local copies, waits for them, and re-layouts  7.57 us (5%)
  other arithmetic  4.37 us (3%)
    pallas_call x1, Pallas kernels, on_device(): pl.pallas_call(body, out_shape=(jax.ShapeDtypeStruct(state.shape, f32), j...  141 us
    unnamed x9, local copies, waits for them, and re-layouts  7.24 us

profile of v1, /device:TPU:1, one launch (start us, length us, event | category | flops | bytes accessed | tf_op | source)
XLA Modules:
  0.0 153.3 jit_solution(4958851645018339540)
XLA Ops:
  0.6 1.3 fusion.24.refs_6_
  1.9 0.5 broadcast.82
  2.5 1.3 reduce.7
  3.8 1.3 reduce.6
  5.2 0.1 reshape.23
  5.3 0.1 reshape.22
  5.4 0.4 fusion.6
  5.8 0.1 copy.18
  5.9 0.6 copy.19
  6.5 140.6 %shard_map.94 = (f32[8,256,512]{2,1,0:T(8,128)}, f32[16,512]{1,0:T(8,128)}, f32[256,512]{1,0:T(8,128)}) custom-call(f32[8,256,512]{2,1,0:T(8,128)} %refs_0_.1, f32[2,256,512]{2,1,0:T(8,128)} %refs_1_.1, s32[256,512]{1,0:T(8,128)} %refs_2_.1, f32[16,512]{1,0:T(8,128)} %refs_3_.1, f32[16,512]{1,0:T(8,128)} %refs_4_.1, s32[1,1024]{1,0:T(1,128)} %bitcast.12, ...), custom_call_target="tpu_custom_call" | custom-call | tf_op jit(solution)/shard_map/pallas_call | solution.py:504
  147.1 0.0 copy-start.1
  147.2 0.0 copy-start
  147.2 4.7 %copy.23 = f32[8,256,512]{2,1,0:T(8,128)} copy(f32[8,256,512]{2,1,0:T(8,128)} %get-tuple-element.6) | data formatting | bytes 8388608
  151.9 0.0 copy-done.1
  151.9 0.6 copy.24
  152.5 0.0 copy-done
  152.5 0.8 copy.25
Async XLA Ops:
  147.1 4.7 %copy-start.1 = (f32[16,512]{1,0:T(8,128)S(1)}, f32[16,512]{1,0:T(8,128)}, u32[]{:S(2)}) copy-start(f32[16,512]{1,0:T(8,128)} %get-tuple-element.7) | copy-start | bytes 98308
  147.2 5.3 %copy-start = (f32[256,512]{1,0:T(8,128)S(1)}, f32[256,512]{1,0:T(8,128)}, u32[]{:S(2)}) copy-start(f32[256,512]{1,0:T(8,128)} %get-tuple-element.8) | copy-start | bytes 1572868

commit v2 on v1

--- a/solution.py
+++ b/solution.py
@@ -35,16 +35,22 @@
     limiter,
     sigma,
     prior,
-    row_target,
-    target,
+    owner,
+    slot,
     out_state,
     out_phi,
     out_foot,
     grid,
     flags,
     fresh,
+    left_x,
+    right_x,
     face_x,
     face_y,
+    face_before,
+    block_at,
+    look_at,
+    look_up_at,
     packs,
     edges,
     corners,
@@ -55,11 +61,13 @@
     dense_sib,
     dense_own,
     got_sib,
+    got_half,
     got_x,
     z_part,
     got_z,
     table,
     foot,
+    look_sem,
     load_sem,
     out_sem,
     send_sem,
@@ -130,14 +138,31 @@
         lanes = slice(128 * j, 128 * j + 128)
         load(("o", j), state.at[: nq - 2, :, lanes], grid.at[: nq - 2, j, mid, :])
 
+    per_row = lon // 128
+    at_owner, at_slot = owner[...], slot[...]
+    look_at[...] = at_owner * sb + at_slot
+    look_load = pltpu.make_async_copy(look_at, look_up_at, look_sem)
+    look_load.start()
+    ordered = (
+        ((at_owner % CORES) * xs + (at_owner // CORES) % xs) * zs + at_owner // (CORES * xs)
+    ) * sb
+    ordered = ordered + (at_slot % per_row) * lat + at_slot // per_row
+    to_lane = lax.broadcasted_iota(jnp.int32, (128, 128), 1)
+    from_lane = lax.broadcasted_iota(jnp.int32, (128, 128), 0)
+    each = 128 // nj
+    moved = ((from_lane % nj) * each + from_lane // nj == to_lane).astype(jnp.float32)
+
+    def move(a):
+        return jnp.dot(a.astype(jnp.float32), moved, preferred_element_type=jnp.float32).astype(jnp.int32)
+
+    block_at[...] = move(ordered // 64) * 64 + move(ordered % 64)
+
     barrier = pltpu.get_barrier_semaphore()
     partners = [*compass.values(), *x_peer.values(), *z_peer.values(), sibling]
     for device in partners:
         pl.semaphore_signal(barrier, inc=1, device_id=device, device_id_type=MESH)
     pl.semaphore_wait(barrier, len(partners))
 
-    lane = lax.broadcasted_iota(jnp.int32, (8, 128), 1)
-    sub = lax.broadcasted_iota(jnp.int32, (8, 128), 0)
 
     for j in range(nj):
         for name in ("f", "v", "l"):
@@ -226,72 +251,77 @@
     unpack(first, 5, 3, corners.at[0], corners.at[1], slice(0, 8), above, 8, GROUPS - 1)
     unpack(first, 5, 3, corners.at[2], corners.at[3], slice(0, 8), below, 8, 0)
 
-    def tile(ref, *at):
-        return ref[at]
+    deep = 16
+    lane_d = lax.broadcasted_iota(jnp.int32, (deep, 128), 1)
 
     def faces(k, carry):
-        b = pl.multiple_of(8 * k, 8)
-        speed_y = [grid[nq + 1, j, pl.ds(b, 8), :] for j in range(nj + 1)]
-        for j, (here, after) in enumerate(zip(speed_y, lane_next(speed_y, lane))):
-            face_y[j, pl.ds(b, 8), :] = 0.2 * (here + after)
-            face_x[j, pl.ds(b, 8), :] = 0.2 * (
-                grid[nq, j, pl.ds(b, 8), :] + grid[nq, j, pl.ds(b + 1, 8), :]
+        b = pl.multiple_of(TOP - 8 + deep * k, 8)
+        speed_y = [grid[nq + 1, j, pl.ds(b, deep), :] for j in range(nj + 1)]
+        faces_y = [0.2 * (here + after) for here, after in zip(speed_y, lane_next(speed_y, lane_d))]
+        faces_before = lane_prev(faces_y, lane_d)
+        for j in range(nj + 1):
+            face_y[j, pl.ds(b, deep), :] = faces_y[j]
+            face_before[j, pl.ds(b, deep), :] = faces_before[j]
+            face_x[j, pl.ds(b, deep), :] = 0.2 * (
+                grid[nq, j, pl.ds(b, deep), :] + grid[nq, j, pl.ds(b + 1, deep), :]
             )
         return carry
 
-    lax.fori_loop(1, TOP // 8 + cx // 8 + 1, faces, 0)
-
-    def advect(q, tiles_x, last):
-        def slopes(k):
-            b = pl.multiple_of(8 * k, 8)
-            lefts, rights = [], []
-            for j in range(tiles_x):
-                here = grid[q, j, pl.ds(b, 8), :]
-                lower = here - grid[q, j, pl.ds(b - 1, 8), :]
-                upper = grid[q, j, pl.ds(b + 1, 8), :] - here
-                half = minmod(lower, upper) * grid[nq + 2, j, pl.ds(b, 8), :]
-                lefts.append(here + half)
-                rights.append(here - half)
-            return tuple(lefts), tuple(pltpu.roll(r, 7, 0) for r in rights)
+    lax.fori_loop(0, (cx + 16) // deep, faces, 0)
+
+    def advect(first_q, tiles_x, start, high, steps):
+        lane_h = lax.broadcasted_iota(jnp.int32, (high, 128), 1)
+
+        def along_x(k, carry):
+            b = pl.multiple_of(TOP - 8 + deep * k, 8)
+            for n in range(2):
+                for j in range(tiles_x):
+                    here = grid[first_q + n, j, pl.ds(b, deep), :]
+                    lower = here - grid[first_q + n, j, pl.ds(b - 1, deep), :]
+                    upper = grid[first_q + n, j, pl.ds(b + 1, deep), :] - here
+                    half = minmod(lower, upper) * grid[nq + 2, j, pl.ds(b, deep), :]
+                    left_x[n, j, pl.ds(b, deep), :] = here + half
+                    right_x[n, j, pl.ds(b, deep), :] = here - half
+            return carry
 
         def step(k, carry):
-            lefts, rights, flux_before = carry
-            lefts_k, rights_k = slopes(k)
-            b = pl.multiple_of(8 * (k - 1), 8)
-            here = [grid[q, j, pl.ds(b, 8), :] for j in range(nj + 1)]
-            diff = [after - h for h, after in zip(here, lane_next(here, lane))]
-            lim = [grid[nq + 2, j, pl.ds(b, 8), :] for j in range(nj + 1)]
-            half = [
-                minmod(lower, upper) * w
-                for lower, upper, w in zip(lane_prev(diff, lane), diff, lim)
-            ]
-            after = lane_next([h - s for h, s in zip(here, half)], lane)
-            flux_y = []
-            for j in range(nj + 1):
-                speed = face_y[j, pl.ds(b, 8), :]
-                flux_y.append(speed * jnp.where(speed > 0.0, here[j] + half[j], after[j]))
-            before_y = lane_prev(flux_y, lane)
-            flux_rolled = []
-            for j in range(tiles_x):
-                speed = face_x[j, pl.ds(b, 8), :]
-                follow = jnp.where(sub == 7, rights_k[j], rights[j])
-                flux = speed * jnp.where(speed > 0.0, lefts[j], follow)
-                rolled = pltpu.roll(flux, 1, 0)
-                flux_rolled.append(rolled)
-                change = (flux - jnp.where(sub == 0, flux_before[j], rolled)) + (
-                    flux_y[j] - before_y[j]
-                )
-                fresh[q, j, pl.ds(b, 8), :] = here[j] - change
-            return lefts_k, rights_k, tuple(flux_rolled)
-
-        zero = tuple(jnp.zeros((8, 128), jnp.float32) for _ in range(tiles_x))
-        lefts, rights = slopes(1)
-        lax.fori_loop(2, last + 1, step, (lefts, rights, zero))
-
-    end = TOP // 8 + cx // 8 + 1
-    advect(nq - 2, nj + 1, end)
-    advect(nq - 1, nj + 1, end)
-
+            b = pl.multiple_of(start + high * k, 8)
+            for n in range(2):
+                here = [grid[first_q + n, j, pl.ds(b, high), :] for j in range(nj + 1)]
+                nexts, befores = lane_next(here, lane_h), lane_prev(here, lane_h)
+                half = [
+                    minmod(h - before, after - h) * grid[nq + 2, j, pl.ds(b, high), :]
+                    for j, (h, before, after) in enumerate(zip(here, befores, nexts))
+                ]
+                left_y = [h + m for h, m in zip(here, half)]
+                right_y = [h - m for h, m in zip(here, half)]
+                right_next, left_before = lane_next(right_y, lane_h), lane_prev(left_y, lane_h)
+                for j in range(tiles_x):
+                    speed = face_y[j, pl.ds(b, high), :]
+                    flux_y = speed * jnp.where(speed > 0.0, left_y[j], right_next[j])
+                    speed = face_before[j, pl.ds(b, high), :]
+                    flux_before = speed * jnp.where(speed > 0.0, left_before[j], right_y[j])
+                    speed = face_x[j, pl.ds(b, high), :]
+                    flux_x = speed * jnp.where(
+                        speed > 0.0,
+                        left_x[n, j, pl.ds(b, high), :],
+                        right_x[n, j, pl.ds(b + 1, high), :],
+                    )
+                    speed = face_x[j, pl.ds(b - 1, high), :]
+                    flux_above = speed * jnp.where(
+                        speed > 0.0,
+                        left_x[n, j, pl.ds(b - 1, high), :],
+                        right_x[n, j, pl.ds(b, high), :],
+                    )
+                    fresh[first_q + n, j, pl.ds(b, high), :] = here[j] - (
+                        (flux_x - flux_above) + (flux_y - flux_before)
+                    )
+            return carry
+
+        lax.fori_loop(0, (cx + 16) // deep, along_x, 0)
+        lax.fori_loop(0, steps, step, 0)
+
+    advect(nq - 2, nj + 1, TOP - 8, deep, (cx + 16) // deep)
     writes = []
 
     def write(src, dst):
@@ -303,7 +333,7 @@
         lanes = slice(128 * j, 128 * j + 128)
         write(fresh.at[nq - 2 : nq, j, mid, :], out_state.at[nq - 2 : nq, :, lanes])
 
-    chunk = 16
+    chunk = each
     lane_c = lax.broadcasted_iota(jnp.int32, (chunk, 128), 1)
 
     def curl(k, carry):
@@ -317,7 +347,7 @@
             ) - 0.5 * (after[j] - before[j])
             high = current.astype(jnp.bfloat16)
             low = (current - high.astype(jnp.float32)).astype(jnp.bfloat16)
-            r = pl.multiple_of(j * cx + chunk * k, chunk)
+            r = pl.multiple_of((k * nj + j) * chunk, chunk)
             weights[pl.ds(r, chunk), 0:128] = high
             weights[pl.ds(r, chunk), 128:256] = low
         return carry
@@ -325,66 +355,89 @@
     lax.fori_loop(0, cx // chunk, curl, 0)
 
     per_x = zs * sb
-    size = min(256, per_x)
+    half = per_x // 2
+    groups = nj * cx // 128
 
     def sums(base, store):
-        def one(i, carry):
-            at = pl.multiple_of(i * size, size)
-            ids = lax.broadcasted_iota(jnp.int32, (size, nj * cx), 0) + (base + at)
-            chosen = jnp.where(ids == row_target[...], 1.0, 0.0).astype(jnp.bfloat16)
-            both = jnp.dot(chosen, weights[...], preferred_element_type=jnp.float32)
-            store[pl.ds(at, size), :] = both[:, :128] + both[:, 128:]
-            return carry
-
-        lax.fori_loop(0, per_x // size, one, 0)
-
-    order = sorted(range(1, xs), key=lambda d: -min(d, xs - d)) + [0]
-    sib_copies, x_copies = {}, {}
+        ids = lax.broadcasted_iota(jnp.int32, (per_x, 128), 0) + base
+        chosen = [
+            jnp.where(ids == block_at[k : k + 1, :], 1.0, 0.0).astype(jnp.bfloat16)
+            for k in range(groups)
+        ]
+        both = jnp.dot(
+            jnp.concatenate(chosen, axis=1), weights[...], preferred_element_type=jnp.float32
+        )
+        store[...] = both[:, :128] + both[:, 128:]
+
+    sib_copies = {}
 
     def for_sibling(d):
-        base = ((1 - core) * xs + lax.rem(at_x + d, xs)) * per_x
-        sums(base, dense_sib.at[d])
+        sums(((1 - core) * xs + lax.rem(at_x + d, xs)) * per_x, dense_sib.at[d])
         sib_copies[d] = send(dense_sib.at[d], got_sib.at[d], sibling)
 
     def for_own(d):
-        base = (core * xs + lax.rem(at_x + d, xs)) * per_x
-        sums(base, dense_own.at[d])
+        sums((core * xs + lax.rem(at_x + d, xs)) * per_x, dense_own.at[d])
         sib_copies[d].wait_recv()
         dense_own[d] = dense_own[d] + got_sib[d]
-        if d:
-            x_copies[d] = send(dense_own.at[d], got_x.at[d - 1], x_peer[d])
-
-    for_sibling(order[0])
-    for i, d in enumerate(order):
-        if i + 1 < len(order):
-            for_sibling(order[i + 1])
-        for_own(d)
-
+
+    def to_x(d, n, part):
+        return send(dense_own.at[d, part, :], got_x.at[n, part, :], x_peer[d])
+
+    first_part, last_part = slice(0, half), slice(half, per_x)
+    if xs == 4:
+        for_sibling(2)
+        for_sibling(1)
+        for_own(2)
+        across_up = send(dense_own.at[2, first_part, :], got_half.at[0], x_peer[1])
+        across_down = send(dense_own.at[2, last_part, :], got_half.at[1], x_peer[3])
+        for_sibling(3)
+        for_own(1)
+        last_in = to_x(1, 0, last_part)
+        for_sibling(0)
+        for_own(3)
+        first_in = to_x(3, 1, first_part)
+        across_up.wait_recv()
+        dense_own[1, first_part, :] = dense_own[1, first_part, :] + got_half[0]
+        x_first = [first_in, to_x(1, 0, first_part)]
+        across_down.wait_recv()
+        dense_own[3, last_part, :] = dense_own[3, last_part, :] + got_half[1]
+        x_last = [last_in, to_x(3, 1, last_part)]
+        for_own(0)
+        terms = 2
+    else:
+        for_sibling(1)
+        for_own(1)
+        x_first = [to_x(1, 0, first_part)]
+        x_last = [to_x(1, 0, last_part)]
+        for_sibling(0)
+        for_own(0)
+        terms = 1
     for copy in halo_o:
         copy.wait_recv()
     for g in range(GROUPS):
         here = slice(TOP + g * rows, TOP + (g + 1) * rows)
         unpack(0, nq - 2, 2, edges_o.at[0], edges_o.at[1], slice(0, rows), here, rows, g)
 
-    def other(q, carry):
-        advect(q, nj, end - 1)
+    def other(n, carry):
+        advect(2 * n, nj, TOP, 32, cx // 32)
         return carry
 
-    lax.fori_loop(0, nq - 2, other, 0)
-    for j in range(nj):
-        lanes = slice(128 * j, 128 * j + 128)
-        write(fresh.at[0 : nq - 2, j, mid, :], out_state.at[0 : nq - 2, :, lanes])
-
-    for copy in x_copies.values():
+    pairs = (nq - 2) // 2
+    lax.fori_loop(0, pairs - 1, other, 0)
+    for copy in x_first + x_last:
         copy.wait_recv()
     total = dense_own[0]
-    for d in range(1, xs):
-        total = total + got_x[d - 1]
+    for n in range(terms):
+        total = total + got_x[n]
     z_part[...] = total
     z_copies = []
     for d in range(1, zs):
         at = pl.multiple_of(lax.rem(at_z + d, zs) * sb, sb)
         z_copies.append(send(z_part.at[pl.ds(at, sb), :], got_z.at[d - 1], z_peer[d]))
+    lax.fori_loop(pairs - 1, pairs, other, 0)
+    for j in range(nj):
+        lanes = slice(128 * j, 128 * j + 128)
+        write(fresh.at[0 : nq - 2, j, mid, :], out_state.at[0 : nq - 2, :, lanes])
     source = z_part[pl.ds(pl.multiple_of(at_z * sb, sb), sb), :]
     for d in range(1, zs):
         z_copies[d - 1].wait_recv()
@@ -424,40 +477,55 @@
     out_phi[...] = phi
 
     def piece(z, x, c):
-        return table.at[pl.ds(pl.multiple_of(((c * xs + x) * zs + z) * sb, sb), sb), :]
-
-    mine = ((core * xs + at_x) * zs + at_z) * sb
-    for c in range(lon // 128):
-        at = pl.multiple_of(mine + c * lat, lat)
-        table[pl.ds(at, lat), :] = phi[:, c * 128 : (c + 1) * 128]
+        return table.at[pl.ds(pl.multiple_of(sec_of(z, x, c) * sb, sb), sb), :]
+
+    mine = pl.multiple_of(me * sb, sb)
+    for c in range(per_row):
+        table[pl.ds(mine + c, lat, stride=per_row), :] = phi[:, c * 128 : (c + 1) * 128]
 
     from_z, from_x, from_sib = {}, {}, []
     own = piece(at_z, at_x, core)
     nearest = sorted(range(1, zs), key=lambda d: min(d, zs - d))
     for d in nearest:
         from_z[d] = send(own, own, z_peer[d])
-    for dz in [0] + nearest:
+    steps = [0] + nearest
+    beside = sorted({1, xs - 1})
+
+    def along_x(i):
+        dz = steps[i]
         if dz:
             from_z[dz].wait_recv()
-        z = lax.rem(at_z + zs - dz, zs)
-        part = piece(z, at_x, core)
-        for dx in range(1, xs):
-            from_x[dz, dx] = send(part, part, x_peer[dx])
+        part = piece(lax.rem(at_z + zs - dz, zs), at_x, core)
+        for dx in beside:
+            from_x[i, dx] = send(part, part, x_peer[dx])
         from_sib.append(send(part, part, sibling))
-    for dz in [0] + nearest:
-        for dx in range(1, xs):
-            from_x[dz, dx].wait_recv()
-            z = lax.rem(at_z + zs - dz, zs)
-            part = piece(z, lax.rem(at_x + xs - dx, xs), core)
-            from_sib.append(send(part, part, sibling))
+
+    def arrived(i, dx):
+        from_x[i, dx].wait_recv()
+        z = lax.rem(at_z + zs - steps[i], zs)
+        part = piece(z, lax.rem(at_x + xs - dx, xs), core)
+        if xs == 4 and dx == (1, 3)[i % 2]:
+            from_x[i, 2] = send(part, part, x_peer[dx])
+        from_sib.append(send(part, part, sibling))
+
+    for i in range(zs + 2):
+        if i < zs:
+            along_x(i)
+        if i >= 2:
+            for dx in beside:
+                arrived(i - 2, dx)
+    if xs == 4:
+        for i in range(zs):
+            arrived(i, 2)
     for copy in from_sib:
         copy.wait_recv()
+    look_load.wait()
 
     def look_up(k, carry):
         b = pl.multiple_of(8 * k, 8)
         for r in range(8):
             for j in range(nj):
-                at = target[(b + r) * nj + j]
+                at = look_up_at[lax.div(b, 128 // nj), lax.rem(b, 128 // nj) * nj + r * nj + j]
                 foot[j, pl.ds(b + r, 1), :] = table[pl.ds(at, 1), :]
         return carry
 
@@ -474,29 +542,22 @@
     state, velocity, limiter, footpoint_owner, footpoint_slot, conductance, potential_prior
 ):
     secs, blks = lax.axis_size("sec"), lax.axis_size("blk")
-    xs = 4 if secs % 8 == 0 and secs >= 32 else 2
+    xs = 4 if secs % 16 == 0 else 2
     zs = secs // (CORES * xs)
     nq, cx, cy = state.shape
     lat, lon = conductance.shape
     nj = cy // 128
     sb = lat * lon // 128
     blocks = nj * cx
-    owner = footpoint_owner.reshape(blocks)
-    slot = footpoint_slot.reshape(blocks)
-    per_row = lon // 128
-    slot = (slot % per_row) * lat + slot // per_row
-    core, x, z = owner % CORES, owner // CORES % xs, owner // (CORES * xs)
-    target = ((core * xs + x) * zs + z) * sb + slot
-    row_target = target.reshape(cx, nj).T.reshape(1, blocks)
-
+    owner = footpoint_owner.reshape(blocks // 128, 128)
+    slot = footpoint_slot.reshape(blocks // 128, 128)
     dims = (zs, xs, secs, blks, nq, cx, cy, lat, lon)
     f32 = jnp.float32
     rows = cx // GROUPS
     per_x = zs * sb
-    messages = 12 + 8 + 8 + xs + (xs - 1) + (zs - 1) + (zs - 1) + zs * (xs - 1) + zs * xs
+    messages = 12 + 8 + 8 + xs + 6 + 2 * (zs - 1) + zs * (xs - 1) + zs * xs
     any_space = pl.BlockSpec(memory_space=pl.ANY)
     vmem = pl.BlockSpec(memory_space=pltpu.VMEM)
-    smem = pl.BlockSpec(memory_space=pltpu.SMEM)
 
     def body(*refs):
         kernel(dims, *refs)
@@ -508,14 +569,20 @@
             jax.ShapeDtypeStruct(conductance.shape, f32),
             jax.ShapeDtypeStruct((cx, cy), f32),
         ),
-        in_specs=[any_space] * 5 + [vmem, smem],
+        in_specs=[any_space] * 5 + [vmem, vmem],
         out_specs=(any_space, vmem, any_space),
         scratch_shapes=[
             pltpu.VMEM((nq + 3, nj + 1, cx + PAD, 128), f32),
             pltpu.VMEM((nj, cx, 128), jnp.int32),
             pltpu.VMEM((nq, nj + 1, cx + PAD, 128), f32),
+            pltpu.VMEM((2, nj + 1, cx + PAD, 128), f32),
+            pltpu.VMEM((2, nj + 1, cx + PAD, 128), f32),
             pltpu.VMEM((nj + 1, cx + PAD, 128), f32),
             pltpu.VMEM((nj + 1, cx + PAD, 128), f32),
+            pltpu.VMEM((nj + 1, cx + PAD, 128), f32),
+            pltpu.VMEM((blocks // 128, 128), jnp.int32),
+            pltpu.VMEM((blocks // 128, 128), jnp.int32),
+            pltpu.SMEM((blocks // 128, 128), jnp.int32),
             pltpu.VMEM((2, rows, 128), f32),
             pltpu.VMEM((2, rows, 128), f32),
             pltpu.VMEM((4, 8, 128), f32),
@@ -526,11 +593,13 @@
             pltpu.VMEM((xs, per_x, 128), f32),
             pltpu.VMEM((xs, per_x, 128), f32),
             pltpu.VMEM((xs, per_x, 128), f32),
-            pltpu.VMEM((xs - 1, per_x, 128), f32),
+            pltpu.VMEM((2, per_x // 2, 128), f32),
+            pltpu.VMEM((2, per_x, 128), f32),
             pltpu.VMEM((per_x, 128), f32),
             pltpu.VMEM((zs - 1, sb, 128), f32),
             pltpu.VMEM((secs * sb, 128), f32),
             pltpu.VMEM((nj, cx, 128), f32),
+            pltpu.SemaphoreType.DMA(()),
             pltpu.SemaphoreType.DMA((4 * nj + 2,)),
             pltpu.SemaphoreType.DMA((3 * nj,)),
             pltpu.SemaphoreType.DMA((messages,)),
@@ -539,7 +608,7 @@
         compiler_params=pltpu.CompilerParams(
             collective_id=0, has_side_effects=True, vmem_limit_bytes=56 * 1024 * 1024
         ),
-    )(state, velocity, limiter, conductance, potential_prior, row_target, target)
+    )(state, velocity, limiter, conductance, potential_prior, owner, slot)
 
 
 def solution(mesh):

time: 154 us -> 85 us (0.55)
  Pallas kernels: 141 us -> 78.1 us
  other arithmetic: 4.37 us -> 0 us
    pallas_call x1, Pallas kernels: 141 us -> 78.1 us  [on_device(): pl.pallas_call(body, out_shape=(jax.ShapeDtypeStruct(state.shape, f32), j...]
    unnamed x2 -> x0, other arithmetic: 2.69 us -> none
    unnamed x9 -> x7, local copies, waits for them, and re-layouts: 7.24 us -> 6.12 us
where the time goes in v2:
time: 85 us; the launch traced here: 84.9 us
  Pallas kernels  78.1 us (92%)
  local copies, waits for them, and re-layouts  6.12 us (7%)
    pallas_call x1, Pallas kernels, on_device(): pl.pallas_call(body, out_shape=(jax.ShapeDtypeStruct(state.shape, f32), j...  78.1 us
    unnamed x7, local copies, waits for them, and re-layouts  6.12 us

profile of v2, /device:TPU:1, one launch (start us, length us, event | category | flops | bytes accessed | tf_op | source)
XLA Modules:
  0.0 84.9 jit_solution(919350319042459859)
XLA Ops:
  0.6 78.1 %shard_map.94 = (f32[8,256,512]{2,1,0:T(8,128)}, f32[16,512]{1,0:T(8,128)}, f32[256,512]{1,0:T(8,128)}) custom-call(f32[8,256,512]{2,1,0:T(8,128)} %refs_0_.1, f32[2,256,512]{2,1,0:T(8,128)} %refs_1_.1, s32[256,512]{1,0:T(8,128)} %refs_2_.1, f32[16,512]{1,0:T(8,128)} %refs_3_.1, f32[16,512]{1,0:T(8,128)} %refs_4_.1, s32[8,128]{1,0:T(8,128)} %bitcast.2, ...), custom_call_target="tpu_custom_call" | custom-call | tf_op jit(solution)/shard_map/pallas_call | solution.py:565
  78.7 0.0 copy-start.1
  78.7 0.0 copy-start
  78.8 4.7 %copy.13 = f32[8,256,512]{2,1,0:T(8,128)} copy(f32[8,256,512]{2,1,0:T(8,128)} %get-tuple-element.6) | data formatting | bytes 8388608
  83.5 0.0 copy-done.1
  83.5 0.6 copy.14
  84.1 0.0 copy-done
  84.1 0.8 copy.15
Async XLA Ops:
  78.7 4.7 %copy-start.1 = (f32[16,512]{1,0:T(8,128)S(1)}, f32[16,512]{1,0:T(8,128)}, u32[]{:S(2)}) copy-start(f32[16,512]{1,0:T(8,128)} %get-tuple-element.7) | copy-start | bytes 98308
  78.7 5.3 %copy-start = (f32[256,512]{1,0:T(8,128)S(1)}, f32[256,512]{1,0:T(8,128)}, u32[]{:S(2)}) copy-start(f32[256,512]{1,0:T(8,128)} %get-tuple-element.8) | copy-start | bytes 1572868

commit v3 on v2

--- a/solution.py
+++ b/solution.py
@@ -61,7 +61,6 @@
     dense_sib,
     dense_own,
     got_sib,
-    got_half,
     got_x,
     z_part,
     got_z,
@@ -144,7 +143,7 @@
     look_load = pltpu.make_async_copy(look_at, look_up_at, look_sem)
     look_load.start()
     ordered = (
-        ((at_owner % CORES) * xs + (at_owner // CORES) % xs) * zs + at_owner // (CORES * xs)
+        ((at_owner % CORES) * zs + at_owner // (CORES * xs)) * xs + (at_owner // CORES) % xs
     ) * sb
     ordered = ordered + (at_slot % per_row) * lat + at_slot // per_row
     to_lane = lax.broadcasted_iota(jnp.int32, (128, 128), 1)
@@ -161,8 +160,6 @@
     partners = [*compass.values(), *x_peer.values(), *z_peer.values(), sibling]
     for device in partners:
         pl.semaphore_signal(barrier, inc=1, device_id=device, device_id_type=MESH)
-    pl.semaphore_wait(barrier, len(partners))
-
 
     for j in range(nj):
         for name in ("f", "v", "l"):
@@ -173,10 +170,6 @@
     fields = slice(first, first + 5)
     top, bottom = slice(TOP, TOP + 8), slice(TOP + cx - 8, TOP + cx)
     above, below = slice(TOP - 8, TOP), slice(TOP + cx, TOP + cx + 8)
-    halo = []
-    halo.append(send(grid.at[fields, 0:nj, bottom, :], grid.at[fields, 0:nj, above, :], (down, col)))
-    halo.append(send(grid.at[fields, 0:nj, top, :], grid.at[fields, 0:nj, below, :], (up, col)))
-
     rows = cx // GROUPS
     wide = lax.broadcasted_iota(jnp.int32, (rows, 128), 1)
 
@@ -204,6 +197,10 @@
     to_left, to_right = pack(first, 5, 3)
     packs[0] = to_left
     packs[1] = to_right
+    pl.semaphore_wait(barrier, len(partners))
+    halo = []
+    halo.append(send(grid.at[fields, 0:nj, bottom, :], grid.at[fields, 0:nj, above, :], (down, col)))
+    halo.append(send(grid.at[fields, 0:nj, top, :], grid.at[fields, 0:nj, below, :], (up, col)))
     halo.append(send(packs.at[1], edges.at[0], (me, right)))
     halo.append(send(packs.at[0], edges.at[1], (me, left)))
     halo.append(send(packs.at[1, rows - 8 : rows, :], corners.at[0], (down, right)))
@@ -251,77 +248,59 @@
     unpack(first, 5, 3, corners.at[0], corners.at[1], slice(0, 8), above, 8, GROUPS - 1)
     unpack(first, 5, 3, corners.at[2], corners.at[3], slice(0, 8), below, 8, 0)
 
-    deep = 16
-    lane_d = lax.broadcasted_iota(jnp.int32, (deep, 128), 1)
-
-    def faces(k, carry):
-        b = pl.multiple_of(TOP - 8 + deep * k, 8)
-        speed_y = [grid[nq + 1, j, pl.ds(b, deep), :] for j in range(nj + 1)]
-        faces_y = [0.2 * (here + after) for here, after in zip(speed_y, lane_next(speed_y, lane_d))]
-        faces_before = lane_prev(faces_y, lane_d)
-        for j in range(nj + 1):
-            face_y[j, pl.ds(b, deep), :] = faces_y[j]
-            face_before[j, pl.ds(b, deep), :] = faces_before[j]
-            face_x[j, pl.ds(b, deep), :] = 0.2 * (
-                grid[nq, j, pl.ds(b, deep), :] + grid[nq, j, pl.ds(b + 1, deep), :]
-            )
-        return carry
-
-    lax.fori_loop(0, (cx + 16) // deep, faces, 0)
-
-    def advect(first_q, tiles_x, start, high, steps):
+    around_rows = cx + 16
+    ring = slice(TOP - 8, TOP + cx + 8)
+    lane_r = lax.broadcasted_iota(jnp.int32, (around_rows, 128), 1)
+    speed_y = [grid[nq + 1, j, ring, :] for j in range(nj + 1)]
+    faces_y = [0.2 * (here + after) for here, after in zip(speed_y, lane_next(speed_y, lane_r))]
+    faces_before = lane_prev(faces_y, lane_r)
+    for j in range(nj + 1):
+        face_y[j, ring, :] = faces_y[j]
+        face_before[j, ring, :] = faces_before[j]
+        face_x[j, ring, :] = 0.2 * (grid[nq, j, ring, :] + grid[nq, j, TOP - 7 : TOP + cx + 9, :])
+
+    def advect(q, tiles_x, start, high):
         lane_h = lax.broadcasted_iota(jnp.int32, (high, 128), 1)
+        deep = 16
 
         def along_x(k, carry):
             b = pl.multiple_of(TOP - 8 + deep * k, 8)
-            for n in range(2):
-                for j in range(tiles_x):
-                    here = grid[first_q + n, j, pl.ds(b, deep), :]
-                    lower = here - grid[first_q + n, j, pl.ds(b - 1, deep), :]
-                    upper = grid[first_q + n, j, pl.ds(b + 1, deep), :] - here
-                    half = minmod(lower, upper) * grid[nq + 2, j, pl.ds(b, deep), :]
-                    left_x[n, j, pl.ds(b, deep), :] = here + half
-                    right_x[n, j, pl.ds(b, deep), :] = here - half
+            for j in range(tiles_x):
+                here = grid[q, j, pl.ds(b, deep), :]
+                lower = here - grid[q, j, pl.ds(b - 1, deep), :]
+                upper = grid[q, j, pl.ds(b + 1, deep), :] - here
+                half = minmod(lower, upper) * grid[nq + 2, j, pl.ds(b, deep), :]
+                left_x[j, pl.ds(b, deep), :] = here + half
+                right_x[j, pl.ds(b, deep), :] = here - half
             return carry
 
-        def step(k, carry):
-            b = pl.multiple_of(start + high * k, 8)
-            for n in range(2):
-                here = [grid[first_q + n, j, pl.ds(b, high), :] for j in range(nj + 1)]
-                nexts, befores = lane_next(here, lane_h), lane_prev(here, lane_h)
-                half = [
-                    minmod(h - before, after - h) * grid[nq + 2, j, pl.ds(b, high), :]
-                    for j, (h, before, after) in enumerate(zip(here, befores, nexts))
-                ]
-                left_y = [h + m for h, m in zip(here, half)]
-                right_y = [h - m for h, m in zip(here, half)]
-                right_next, left_before = lane_next(right_y, lane_h), lane_prev(left_y, lane_h)
-                for j in range(tiles_x):
-                    speed = face_y[j, pl.ds(b, high), :]
-                    flux_y = speed * jnp.where(speed > 0.0, left_y[j], right_next[j])
-                    speed = face_before[j, pl.ds(b, high), :]
-                    flux_before = speed * jnp.where(speed > 0.0, left_before[j], right_y[j])
-                    speed = face_x[j, pl.ds(b, high), :]
-                    flux_x = speed * jnp.where(
-                        speed > 0.0,
-                        left_x[n, j, pl.ds(b, high), :],
-                        right_x[n, j, pl.ds(b + 1, high), :],
-                    )
-                    speed = face_x[j, pl.ds(b - 1, high), :]
-                    flux_above = speed * jnp.where(
-                        speed > 0.0,
-                        left_x[n, j, pl.ds(b - 1, high), :],
-                        right_x[n, j, pl.ds(b, high), :],
-                    )
-                    fresh[first_q + n, j, pl.ds(b, high), :] = here[j] - (
-                        (flux_x - flux_above) + (flux_y - flux_before)
-                    )
-            return carry
-
         lax.fori_loop(0, (cx + 16) // deep, along_x, 0)
-        lax.fori_loop(0, steps, step, 0)
-
-    advect(nq - 2, nj + 1, TOP - 8, deep, (cx + 16) // deep)
+        at, above, below = (slice(start + n, start + n + high) for n in (0, -1, 1))
+        here = [grid[q, j, at, :] for j in range(nj + 1)]
+        nexts, befores = lane_next(here, lane_h), lane_prev(here, lane_h)
+        half = [
+            minmod(h - before, after - h) * grid[nq + 2, j, at, :]
+            for j, (h, before, after) in enumerate(zip(here, befores, nexts))
+        ]
+        left_y = [h + m for h, m in zip(here, half)]
+        right_y = [h - m for h, m in zip(here, half)]
+        right_next, left_before = lane_next(right_y, lane_h), lane_prev(left_y, lane_h)
+        for j in range(tiles_x):
+            speed = face_y[j, at, :]
+            flux_y = speed * jnp.where(speed > 0.0, left_y[j], right_next[j])
+            speed = face_before[j, at, :]
+            flux_before = speed * jnp.where(speed > 0.0, left_before[j], right_y[j])
+            speed = face_x[j, at, :]
+            flux_x = speed * jnp.where(speed > 0.0, left_x[j, at, :], right_x[j, below, :])
+            speed = face_x[j, above, :]
+            flux_above = speed * jnp.where(speed > 0.0, left_x[j, above, :], right_x[j, at, :])
+            fresh[q, j, at, :] = here[j] - ((flux_x - flux_above) + (flux_y - flux_before))
+
+    def field(q, carry):
+        advect(q, nj + 1, TOP - 8, cx + 16)
+        return carry
+
+    lax.fori_loop(nq - 2, nq, field, 0)
     writes = []
 
     def write(src, dst):
@@ -333,33 +312,34 @@
         lanes = slice(128 * j, 128 * j + 128)
         write(fresh.at[nq - 2 : nq, j, mid, :], out_state.at[nq - 2 : nq, :, lanes])
 
-    chunk = each
-    lane_c = lax.broadcasted_iota(jnp.int32, (chunk, 128), 1)
-
-    def curl(k, carry):
-        b = pl.multiple_of(TOP + chunk * k, 8)
-        field_x = [fresh[nq - 2, j, pl.ds(b, chunk), :] for j in range(nj + 1)]
-        after = lane_next(field_x, lane_c)
-        before = lane_prev(field_x, lane_c)
-        for j in range(nj):
-            current = 0.5 * (
-                fresh[nq - 1, j, pl.ds(b + 1, chunk), :] - fresh[nq - 1, j, pl.ds(b - 1, chunk), :]
-            ) - 0.5 * (after[j] - before[j])
-            high = current.astype(jnp.bfloat16)
-            low = (current - high.astype(jnp.float32)).astype(jnp.bfloat16)
-            r = pl.multiple_of((k * nj + j) * chunk, chunk)
-            weights[pl.ds(r, chunk), 0:128] = high
-            weights[pl.ds(r, chunk), 128:256] = low
-        return carry
-
-    lax.fori_loop(0, cx // chunk, curl, 0)
-
-    per_x = zs * sb
-    half = per_x // 2
+    lane_c = lax.broadcasted_iota(jnp.int32, (cx, 128), 1)
+    field_x = [fresh[nq - 2, j, mid, :] for j in range(nj + 1)]
+    after, before = lane_next(field_x, lane_c), lane_prev(field_x, lane_c)
+    for j in range(nj):
+        current = 0.5 * (
+            fresh[nq - 1, j, TOP + 1 : TOP + cx + 1, :] - fresh[nq - 1, j, TOP - 1 : TOP + cx - 1, :]
+        ) - 0.5 * (after[j] - before[j])
+        high = current.astype(jnp.bfloat16)
+        low = (current - high.astype(jnp.float32)).astype(jnp.bfloat16)
+        for k in range(cx // each):
+            part = slice((k * nj + j) * each, (k * nj + j + 1) * each)
+            weights[part, 0:128] = high[k * each : (k + 1) * each, :]
+            weights[part, 128:256] = low[k * each : (k + 1) * each, :]
+
+    order = sorted(range(zs), key=lambda d: -min(d, zs - d))
+    duos = [order[n : n + 2] for n in range(0, zs, 2)]
+    per_z = xs * sb
     groups = nj * cx // 128
 
-    def sums(base, store):
-        ids = lax.broadcasted_iota(jnp.int32, (per_x, 128), 0) + base
+    def sums(duo, to_core):
+        ids = jnp.concatenate(
+            [
+                lax.broadcasted_iota(jnp.int32, (per_z, 128), 0)
+                + (to_core * zs + lax.rem(at_z + d, zs)) * per_z
+                for d in duo
+            ],
+            axis=0,
+        )
         chosen = [
             jnp.where(ids == block_at[k : k + 1, :], 1.0, 0.0).astype(jnp.bfloat16)
             for k in range(groups)
@@ -367,80 +347,60 @@
         both = jnp.dot(
             jnp.concatenate(chosen, axis=1), weights[...], preferred_element_type=jnp.float32
         )
-        store[...] = both[:, :128] + both[:, 128:]
-
-    sib_copies = {}
-
-    def for_sibling(d):
-        sums(((1 - core) * xs + lax.rem(at_x + d, xs)) * per_x, dense_sib.at[d])
-        sib_copies[d] = send(dense_sib.at[d], got_sib.at[d], sibling)
-
-    def for_own(d):
-        sums((core * xs + lax.rem(at_x + d, xs)) * per_x, dense_own.at[d])
-        sib_copies[d].wait_recv()
-        dense_own[d] = dense_own[d] + got_sib[d]
-
-    def to_x(d, n, part):
-        return send(dense_own.at[d, part, :], got_x.at[n, part, :], x_peer[d])
-
-    first_part, last_part = slice(0, half), slice(half, per_x)
-    if xs == 4:
-        for_sibling(2)
-        for_sibling(1)
-        for_own(2)
-        across_up = send(dense_own.at[2, first_part, :], got_half.at[0], x_peer[1])
-        across_down = send(dense_own.at[2, last_part, :], got_half.at[1], x_peer[3])
-        for_sibling(3)
-        for_own(1)
-        last_in = to_x(1, 0, last_part)
-        for_sibling(0)
-        for_own(3)
-        first_in = to_x(3, 1, first_part)
-        across_up.wait_recv()
-        dense_own[1, first_part, :] = dense_own[1, first_part, :] + got_half[0]
-        x_first = [first_in, to_x(1, 0, first_part)]
-        across_down.wait_recv()
-        dense_own[3, last_part, :] = dense_own[3, last_part, :] + got_half[1]
-        x_last = [last_in, to_x(3, 1, last_part)]
-        for_own(0)
-        terms = 2
-    else:
-        for_sibling(1)
-        for_own(1)
-        x_first = [to_x(1, 0, first_part)]
-        x_last = [to_x(1, 0, last_part)]
-        for_sibling(0)
-        for_own(0)
-        terms = 1
+        return (both[:, :128] + both[:, 128:]).reshape(2, xs, sb, 128)
+
+    sib_copies, x_copies, z_copies = {}, {}, {}
+
+    def for_sibling(n):
+        dense_sib[n] = sums(duos[n], 1 - core)
+        sib_copies[n] = send(dense_sib.at[n], got_sib.at[n], sibling)
+
+    def for_own(n):
+        dense_own[n] = sums(duos[n], core)
+        sib_copies[n].wait_recv()
+        dense_own[n] = dense_own[n] + got_sib[n]
+        for d in sorted(x_peer, key=lambda d: -min(d, xs - d)):
+            part = dense_own.at[n, :, lax.rem(at_x + d, xs)]
+            x_copies[n, d] = send(part, got_x.at[n, d - 1], x_peer[d])
+
+    for_sibling(0)
+    for n in range(len(duos)):
+        if n + 1 < len(duos):
+            for_sibling(n + 1)
+        for_own(n)
     for copy in halo_o:
         copy.wait_recv()
     for g in range(GROUPS):
         here = slice(TOP + g * rows, TOP + (g + 1) * rows)
         unpack(0, nq - 2, 2, edges_o.at[0], edges_o.at[1], slice(0, rows), here, rows, g)
 
-    def other(n, carry):
-        advect(2 * n, nj, TOP, 32, cx // 32)
+    def other(q, carry):
+        advect(q, nj, TOP, cx)
         return carry
 
-    pairs = (nq - 2) // 2
-    lax.fori_loop(0, pairs - 1, other, 0)
-    for copy in x_first + x_last:
-        copy.wait_recv()
-    total = dense_own[0]
-    for n in range(terms):
-        total = total + got_x[n]
-    z_part[...] = total
-    z_copies = []
-    for d in range(1, zs):
-        at = pl.multiple_of(lax.rem(at_z + d, zs) * sb, sb)
-        z_copies.append(send(z_part.at[pl.ds(at, sb), :], got_z.at[d - 1], z_peer[d]))
-    lax.fori_loop(pairs - 1, pairs, other, 0)
+    def along_z(n):
+        for d in x_peer:
+            x_copies[n, d].wait_recv()
+        for h, d in enumerate(duos[n]):
+            part = dense_own[n, h, at_x]
+            for e in x_peer:
+                part = part + got_x[n, e - 1, h]
+            z_part[n, h] = part
+            if d:
+                z_copies[d] = send(z_part.at[n, h], got_z.at[d - 1], z_peer[d])
+
+    done = (nq - 2) // 2
+    lax.fori_loop(0, done, other, 0)
+    for n in range(len(duos)):
+        if n == len(duos) - 1:
+            lax.fori_loop(done, nq - 2, other, 0)
+        along_z(n)
     for j in range(nj):
         lanes = slice(128 * j, 128 * j + 128)
         write(fresh.at[0 : nq - 2, j, mid, :], out_state.at[0 : nq - 2, :, lanes])
-    source = z_part[pl.ds(pl.multiple_of(at_z * sb, sb), sb), :]
-    for d in range(1, zs):
-        z_copies[d - 1].wait_recv()
+    source = z_part[len(duos) - 1, 1]
+    for d in order[:-1]:
+        z_copies[d].wait_recv()
         source = source + got_z[d - 1]
     for c in range(lon // 128):
         at = 128 + 128 * c
@@ -489,34 +449,25 @@
     for d in nearest:
         from_z[d] = send(own, own, z_peer[d])
     steps = [0] + nearest
-    beside = sorted({1, xs - 1})
+    order_x = sorted(x_peer, key=lambda d: -min(d, xs - d))
 
     def along_x(i):
         dz = steps[i]
         if dz:
             from_z[dz].wait_recv()
         part = piece(lax.rem(at_z + zs - dz, zs), at_x, core)
-        for dx in beside:
+        for dx in order_x:
             from_x[i, dx] = send(part, part, x_peer[dx])
         from_sib.append(send(part, part, sibling))
 
-    def arrived(i, dx):
-        from_x[i, dx].wait_recv()
-        z = lax.rem(at_z + zs - steps[i], zs)
-        part = piece(z, lax.rem(at_x + xs - dx, xs), core)
-        if xs == 4 and dx == (1, 3)[i % 2]:
-            from_x[i, 2] = send(part, part, x_peer[dx])
-        from_sib.append(send(part, part, sibling))
-
-    for i in range(zs + 2):
-        if i < zs:
-            along_x(i)
-        if i >= 2:
-            for dx in beside:
-                arrived(i - 2, dx)
-    if xs == 4:
-        for i in range(zs):
-            arrived(i, 2)
+    for i in range(zs):
+        along_x(i)
+    for i in range(zs):
+        for dx in order_x:
+            from_x[i, dx].wait_recv()
+            z = lax.rem(at_z + zs - steps[i], zs)
+            part = piece(z, lax.rem(at_x + xs - dx, xs), core)
+            from_sib.append(send(part, part, sibling))
     for copy in from_sib:
         copy.wait_recv()
     look_load.wait()
@@ -554,8 +505,7 @@
     dims = (zs, xs, secs, blks, nq, cx, cy, lat, lon)
     f32 = jnp.float32
     rows = cx // GROUPS
-    per_x = zs * sb
-    messages = 12 + 8 + 8 + xs + 6 + 2 * (zs - 1) + zs * (xs - 1) + zs * xs
+    messages = 12 + 8 + 8 + zs // 2 + zs // 2 * (xs - 1) + 2 * (zs - 1) + zs * (xs - 1) + zs * xs
     any_space = pl.BlockSpec(memory_space=pl.ANY)
     vmem = pl.BlockSpec(memory_space=pltpu.VMEM)
 
@@ -575,8 +525,8 @@
             pltpu.VMEM((nq + 3, nj + 1, cx + PAD, 128), f32),
             pltpu.VMEM((nj, cx, 128), jnp.int32),
             pltpu.VMEM((nq, nj + 1, cx + PAD, 128), f32),
-            pltpu.VMEM((2, nj + 1, cx + PAD, 128), f32),
-            pltpu.VMEM((2, nj + 1, cx + PAD, 128), f32),
+            pltpu.VMEM((nj + 1, cx + PAD, 128), f32),
+            pltpu.VMEM((nj + 1, cx + PAD, 128), f32),
             pltpu.VMEM((nj + 1, cx + PAD, 128), f32),
             pltpu.VMEM((nj + 1, cx + PAD, 128), f32),
             pltpu.VMEM((nj + 1, cx + PAD, 128), f32),
@@ -590,12 +540,11 @@
             pltpu.VMEM((2, rows, 128), f32),
             pltpu.VMEM((3, lat + 16, lon + 256), f32),
             pltpu.VMEM((blocks, 256), jnp.bfloat16),
-            pltpu.VMEM((xs, per_x, 128), f32),
-            pltpu.VMEM((xs, per_x, 128), f32),
-            pltpu.VMEM((xs, per_x, 128), f32),
-            pltpu.VMEM((2, per_x // 2, 128), f32),
-            pltpu.VMEM((2, per_x, 128), f32),
-            pltpu.VMEM((per_x, 128), f32),
+            pltpu.VMEM((zs // 2, 2, xs, sb, 128), f32),
+            pltpu.VMEM((zs // 2, 2, xs, sb, 128), f32),
+            pltpu.VMEM((zs // 2, 2, xs, sb, 128), f32),
+            pltpu.VMEM((zs // 2, xs - 1, 2, sb, 128), f32),
+            pltpu.VMEM((zs // 2, 2, sb, 128), f32),
             pltpu.VMEM((zs - 1, sb, 128), f32),
             pltpu.VMEM((secs * sb, 128), f32),
             pltpu.VMEM((nj, cx, 128), f32),

time: 85 us -> 77.7 us (0.914)
  Pallas kernels: 78.1 us -> 70.8 us
    pallas_call x1, Pallas kernels: 78.1 us -> 70.8 us  [on_device(): pl.pallas_call(body, out_shape=(jax.ShapeDtypeStruct(state.shape, f32), j...]
where the time goes in v3:
time: 77.7 us; the launch traced here: 77.6 us
  Pallas kernels  70.8 us (91%)
  local copies, waits for them, and re-layouts  6.12 us (8%)
    pallas_call x1, Pallas kernels, on_device(): pl.pallas_call(body, out_shape=(jax.ShapeDtypeStruct(state.shape, f32), j...  70.8 us
    unnamed x7, local copies, waits for them, and re-layouts  6.12 us

profile of v3, /device:TPU:1, one launch (start us, length us, event | category | flops | bytes accessed | tf_op | source)
XLA Modules:
  0.0 77.6 jit_solution(15397856685031406561)
XLA Ops:
  0.6 70.8 %shard_map.94 = (f32[8,256,512]{2,1,0:T(8,128)}, f32[16,512]{1,0:T(8,128)}, f32[256,512]{1,0:T(8,128)}) custom-call(f32[8,256,512]{2,1,0:T(8,128)} %refs_0_.1, f32[2,256,512]{2,1,0:T(8,128)} %refs_1_.1, s32[256,512]{1,0:T(8,128)} %refs_2_.1, f32[16,512]{1,0:T(8,128)} %refs_3_.1, f32[16,512]{1,0:T(8,128)} %refs_4_.1, s32[8,128]{1,0:T(8,128)} %bitcast.2, ...), custom_call_target="tpu_custom_call" | custom-call | tf_op jit(solution)/shard_map/pallas_call | solution.py:515
  71.4 0.0 copy-start.1
  71.4 0.0 copy-start
  71.5 4.7 %copy.13 = f32[8,256,512]{2,1,0:T(8,128)} copy(f32[8,256,512]{2,1,0:T(8,128)} %get-tuple-element.6) | data formatting | bytes 8388608
  76.2 0.0 copy-done.1
  76.2 0.6 copy.14
  76.8 0.0 copy-done
  76.8 0.8 %copy.15 = f32[256,512]{1,0:T(8,128)} copy(f32[256,512]{1,0:T(8,128)S(1)} %copy-done) | data formatting | bytes 1048576
Async XLA Ops:
  71.4 4.7 %copy-start.1 = (f32[16,512]{1,0:T(8,128)S(1)}, f32[16,512]{1,0:T(8,128)}, u32[]{:S(2)}) copy-start(f32[16,512]{1,0:T(8,128)} %get-tuple-element.7) | copy-start | bytes 98308
  71.4 5.3 %copy-start = (f32[256,512]{1,0:T(8,128)S(1)}, f32[256,512]{1,0:T(8,128)}, u32[]{:S(2)}) copy-start(f32[256,512]{1,0:T(8,128)} %get-tuple-element.8) | copy-start | bytes 1572868

commit v4 on v3

--- a/solution.py
+++ b/solution.py
@@ -37,17 +37,17 @@
     prior,
     owner,
     slot,
-    out_state,
+    fresh,
     out_phi,
-    out_foot,
+    foot,
     grid,
     flags,
-    fresh,
     left_x,
     right_x,
     face_x,
     face_y,
     face_before,
+    blocks_to,
     block_at,
     look_at,
     look_up_at,
@@ -65,10 +65,8 @@
     z_part,
     got_z,
     table,
-    foot,
     look_sem,
     load_sem,
-    out_sem,
     send_sem,
     recv_sem,
 ):
@@ -118,6 +116,11 @@
         sent.append(copy)
         return copy
 
+    barrier = pltpu.get_barrier_semaphore()
+    partners = [*compass.values(), *x_peer.values(), *z_peer.values(), sibling]
+    for device in partners:
+        pl.semaphore_signal(barrier, inc=1, device_id=device, device_id_type=MESH)
+
     loads = {}
 
     def load(name, src, dst):
@@ -125,6 +128,8 @@
         copy.start()
         loads[name] = copy
 
+    load("owner", owner, blocks_to.at[0])
+    load("slot", slot, blocks_to.at[1])
     mid = slice(TOP, TOP + cx)
     for j in range(nj):
         lanes = slice(128 * j, 128 * j + 128)
@@ -138,7 +143,9 @@
         load(("o", j), state.at[: nq - 2, :, lanes], grid.at[: nq - 2, j, mid, :])
 
     per_row = lon // 128
-    at_owner, at_slot = owner[...], slot[...]
+    loads["owner"].wait()
+    loads["slot"].wait()
+    at_owner, at_slot = blocks_to[0], blocks_to[1]
     look_at[...] = at_owner * sb + at_slot
     look_load = pltpu.make_async_copy(look_at, look_up_at, look_sem)
     look_load.start()
@@ -155,11 +162,6 @@
         return jnp.dot(a.astype(jnp.float32), moved, preferred_element_type=jnp.float32).astype(jnp.int32)
 
     block_at[...] = move(ordered // 64) * 64 + move(ordered % 64)
-
-    barrier = pltpu.get_barrier_semaphore()
-    partners = [*compass.values(), *x_peer.values(), *z_peer.values(), sibling]
-    for device in partners:
-        pl.semaphore_signal(barrier, inc=1, device_id=device, device_id_type=MESH)
 
     for j in range(nj):
         for name in ("f", "v", "l"):
@@ -301,17 +303,6 @@
         return carry
 
     lax.fori_loop(nq - 2, nq, field, 0)
-    writes = []
-
-    def write(src, dst):
-        copy = pltpu.make_async_copy(src, dst, out_sem.at[len(writes)])
-        copy.start()
-        writes.append(copy)
-
-    for j in range(nj):
-        lanes = slice(128 * j, 128 * j + 128)
-        write(fresh.at[nq - 2 : nq, j, mid, :], out_state.at[nq - 2 : nq, :, lanes])
-
     lane_c = lax.broadcasted_iota(jnp.int32, (cx, 128), 1)
     field_x = [fresh[nq - 2, j, mid, :] for j in range(nj + 1)]
     after, before = lane_next(field_x, lane_c), lane_prev(field_x, lane_c)
@@ -395,9 +386,6 @@
         if n == len(duos) - 1:
             lax.fori_loop(done, nq - 2, other, 0)
         along_z(n)
-    for j in range(nj):
-        lanes = slice(128 * j, 128 * j + 128)
-        write(fresh.at[0 : nq - 2, j, mid, :], out_state.at[0 : nq - 2, :, lanes])
     source = z_part[len(duos) - 1, 1]
     for d in order[:-1]:
         z_copies[d].wait_recv()
@@ -481,11 +469,21 @@
         return carry
 
     lax.fori_loop(0, cx // 8, look_up, 0)
-    for j in range(nj):
-        write(foot.at[j], out_foot.at[:, 128 * j : 128 * j + 128])
     for copy in sent:
         copy.wait_send()
-    for copy in writes:
+
+
+def write_out(fresh, phi, foot, out_state, out_phi, out_foot, sem):
+    cx = foot.shape[1]
+    copies = [pltpu.make_async_copy(phi, out_phi, sem.at[0])]
+    for j in range(foot.shape[0]):
+        lanes = slice(128 * j, 128 * j + 128)
+        mid = fresh.at[:, j, TOP : TOP + cx, :]
+        copies.append(pltpu.make_async_copy(mid, out_state.at[:, :, lanes], sem.at[2 * j + 1]))
+        copies.append(pltpu.make_async_copy(foot.at[j], out_foot.at[:, lanes], sem.at[2 * j + 2]))
+    for copy in copies:
+        copy.start()
+    for copy in copies:
         copy.wait()
 
 
@@ -512,24 +510,24 @@
     def body(*refs):
         kernel(dims, *refs)
 
-    return pl.pallas_call(
+    results = pl.pallas_call(
         body,
         out_shape=(
-            jax.ShapeDtypeStruct(state.shape, f32),
-            jax.ShapeDtypeStruct(conductance.shape, f32),
-            jax.ShapeDtypeStruct((cx, cy), f32),
+            pltpu.VMEM((nq, nj + 1, cx + PAD, 128), f32),
+            pltpu.VMEM(conductance.shape, f32),
+            pltpu.VMEM((nj, cx, 128), f32),
         ),
-        in_specs=[any_space] * 5 + [vmem, vmem],
-        out_specs=(any_space, vmem, any_space),
+        in_specs=[pl.BlockSpec(memory_space=pltpu.HBM)] * 7,
+        out_specs=(vmem, vmem, vmem),
         scratch_shapes=[
             pltpu.VMEM((nq + 3, nj + 1, cx + PAD, 128), f32),
             pltpu.VMEM((nj, cx, 128), jnp.int32),
-            pltpu.VMEM((nq, nj + 1, cx + PAD, 128), f32),
             pltpu.VMEM((nj + 1, cx + PAD, 128), f32),
             pltpu.VMEM((nj + 1, cx + PAD, 128), f32),
             pltpu.VMEM((nj + 1, cx + PAD, 128), f32),
             pltpu.VMEM((nj + 1, cx + PAD, 128), f32),
             pltpu.VMEM((nj + 1, cx + PAD, 128), f32),
+            pltpu.VMEM((2, blocks // 128, 128), jnp.int32),
             pltpu.VMEM((blocks // 128, 128), jnp.int32),
             pltpu.VMEM((blocks // 128, 128), jnp.int32),
             pltpu.SMEM((blocks // 128, 128), jnp.int32),
@@ -547,17 +545,32 @@
             pltpu.VMEM((zs // 2, 2, sb, 128), f32),
             pltpu.VMEM((zs - 1, sb, 128), f32),
             pltpu.VMEM((secs * sb, 128), f32),
-            pltpu.VMEM((nj, cx, 128), f32),
             pltpu.SemaphoreType.DMA(()),
-            pltpu.SemaphoreType.DMA((4 * nj + 2,)),
-            pltpu.SemaphoreType.DMA((3 * nj,)),
+            pltpu.SemaphoreType.DMA((4 * nj + 4,)),
             pltpu.SemaphoreType.DMA((messages,)),
             pltpu.SemaphoreType.DMA((messages,)),
         ],
         compiler_params=pltpu.CompilerParams(
-            collective_id=0, has_side_effects=True, vmem_limit_bytes=56 * 1024 * 1024
+            collective_id=0, has_side_effects=True, vmem_limit_bytes=40 * 1024 * 1024
         ),
-    )(state, velocity, limiter, conductance, potential_prior, owner, slot)
+    )(
+        *[
+            pltpu.with_memory_space_constraint(a, pltpu.HBM)
+            for a in (state, velocity, limiter, conductance, potential_prior, owner, slot)
+        ],
+    )
+    return pl.pallas_call(
+        write_out,
+        out_shape=(
+            jax.ShapeDtypeStruct(state.shape, f32),
+            jax.ShapeDtypeStruct(conductance.shape, f32),
+            jax.ShapeDtypeStruct((cx, cy), f32),
+        ),
+        in_specs=[vmem] * 3,
+        out_specs=(any_space,) * 3,
+        scratch_shapes=[pltpu.SemaphoreType.DMA((2 * nj + 1,))],
+        compiler_params=pltpu.CompilerParams(vmem_limit_bytes=16 * 1024 * 1024),
+    )(*[pltpu.with_memory_space_constraint(r, pltpu.VMEM) for r in results])
 
 
 def solution(mesh):

time: 77.7 us -> 71.5 us (0.920)
  local copies, waits for them, and re-layouts: 6.12 us -> 0 us
    unnamed x7 -> x0, local copies, waits for them, and re-layouts: 6.12 us -> none
    pallas_call x1 -> x2, Pallas kernels: 70.8 us -> 70.8 us  [the longest x1 68.5 us: on_device(): pl.pallas_call(body, out_shape=(pltpu.VMEM((nq, nj + 1, cx + PAD, 128), f...]
where the time goes in v4:
time: 71.5 us; the launch traced here: 71.4 us
  Pallas kernels  70.8 us (99%)
    pallas_call x1, Pallas kernels, on_device(): pl.pallas_call(body, out_shape=(pltpu.VMEM((nq, nj + 1, cx + PAD, 128), f...  68.5 us
    pallas_call x1, Pallas kernels, on_device(): pl.pallas_call(write_out, out_shape=(jax.ShapeDtypeStruct(state.shape, f3...  2.26 us

profile of v4, /device:TPU:1, one launch (start us, length us, event | category | flops | bytes accessed | tf_op | source)
XLA Modules:
  0.0 71.4 jit_solution(12233931243553149175)
XLA Ops:
  0.6 68.5 %shard_map.94 = (f32[8,5,296,128]{3,2,1,0:T(8,128)S(1)}, f32[16,512]{1,0:T(8,128)S(1)}, f32[4,256,128]{2,1,0:T(8,128)S(1)}) custom-call(f32[8,256,512]{2,1,0:T(8,128)} %refs_0_.1, f32[2,256,512]{2,1,0:T(8,128)} %refs_1_.1, s32[256,512]{1,0:T(8,128)} %refs_2_.1, f32[16,512]{1,0:T(8,128)} %refs_3_.1, f32[16,512]{1,0:T(8,128)} %refs_4_.1, s32[8,128]{1,0:T(8,128)} %bitcast.2, ...), custom_call_target="tpu_custom_call" | custom-call | tf_op jit(solution)/shard_map/pallas_call | solution.py:513
  69.2 2.3 %shard_map.95 = (f32[8,256,512]{2,1,0:T(8,128)}, f32[16,512]{1,0:T(8,128)}, f32[256,512]{1,0:T(8,128)}) custom-call(f32[8,5,296,128]{3,2,1,0:T(8,128)S(1)} %get-tuple-element.6.fresh, f32[16,512]{1,0:T(8,128)S(1)} %get-tuple-element.7.phi, f32[4,256,128]{2,1,0:T(8,128)S(1)} %get-tuple-element.8.foot), custom_call_target="tpu_custom_call" | custom-call | tf_op jit(solution)/shard_map/pallas_call | solution.py:562

commit v5 on v4

--- a/solution.py
+++ b/solution.py
@@ -128,19 +128,85 @@
         copy.start()
         loads[name] = copy
 
-    load("owner", owner, blocks_to.at[0])
-    load("slot", slot, blocks_to.at[1])
     mid = slice(TOP, TOP + cx)
     for j in range(nj):
         lanes = slice(128 * j, 128 * j + 128)
         load(("f", j), state.at[nq - 2 : nq, :, lanes], grid.at[nq - 2 : nq, j, mid, :])
         load(("v", j), velocity.at[:, :, lanes], grid.at[nq : nq + 2, j, mid, :])
         load(("l", j), limiter.at[:, lanes], flags.at[j])
+    load("owner", owner, blocks_to.at[0])
+    load("slot", slot, blocks_to.at[1])
     load("sigma", sigma, shell.at[0, 8 : 8 + lat, 128 : 128 + lon])
     load("prior", prior, shell.at[1, 8 : 8 + lat, 128 : 128 + lon])
     for j in range(nj):
         lanes = slice(128 * j, 128 * j + 128)
         load(("o", j), state.at[: nq - 2, :, lanes], grid.at[: nq - 2, j, mid, :])
+
+    for j in range(nj):
+        for name in ("f", "v", "l"):
+            loads[(name, j)].wait()
+    for j in range(nj):
+        grid[nq + 2, j, mid, :] = 0.5 * flags[j].astype(jnp.float32)
+    first = nq - 2
+    fields = slice(first, first + 5)
+    top, bottom = slice(TOP, TOP + 8), slice(TOP + cx - 8, TOP + cx)
+    above, below = slice(TOP - 8, TOP), slice(TOP + cx, TOP + cx + 8)
+    rows = cx // GROUPS
+    wide = lax.broadcasted_iota(jnp.int32, (rows, 128), 1)
+
+    def pack(base, count, width):
+        at_left = jnp.zeros((rows, 128), jnp.float32)
+        at_right = jnp.zeros((rows, 128), jnp.float32)
+        for g in range(GROUPS):
+            here = slice(TOP + g * rows, TOP + (g + 1) * rows)
+            for a in range(count):
+                at = 16 * g + width * a
+                mask = (wide >= at) & (wide < at + width)
+                at_left = jnp.where(mask, pltpu.roll(grid[base + a, 0, here, :], at, 1), at_left)
+                moved = pltpu.roll(grid[base + a, nj - 1, here, :], (at + width) % 128, 1)
+                at_right = jnp.where(mask, moved, at_right)
+        return at_left, at_right
+
+    def unpack(base, count, width, from_left, from_right, take, put, size, group):
+        side = lax.broadcasted_iota(jnp.int32, (size, 128), 1) < 64
+        for a in range(count):
+            at = 16 * group + width * a
+            r = pltpu.roll(from_right[take, :], (128 - at) % 128, 1)
+            l = pltpu.roll(from_left[take, :], (256 - width - at) % 128, 1)
+            grid[base + a, nj, put, :] = jnp.where(side, r, l)
+
+    to_left, to_right = pack(first, 5, 3)
+    packs[0] = to_left
+    packs[1] = to_right
+    pl.semaphore_wait(barrier, len(partners))
+    halo = []
+    halo.append(send(grid.at[fields, 0:nj, bottom, :], grid.at[fields, 0:nj, above, :], (down, col)))
+    halo.append(send(grid.at[fields, 0:nj, top, :], grid.at[fields, 0:nj, below, :], (up, col)))
+    halo.append(send(packs.at[1], edges.at[0], (me, right)))
+    halo.append(send(packs.at[0], edges.at[1], (me, left)))
+    halo.append(send(packs.at[1, rows - 8 : rows, :], corners.at[0], (down, right)))
+    halo.append(send(packs.at[0, rows - 8 : rows, :], corners.at[1], (down, left)))
+    halo.append(send(packs.at[1, 0:8, :], corners.at[2], (up, right)))
+    halo.append(send(packs.at[0, 0:8, :], corners.at[3], (up, left)))
+
+    row_src = {0: slice(8, 8 + lat), 1: slice(lat, lat + 8), -1: slice(8, 16)}
+    row_dst = {0: slice(8, 8 + lat), 1: slice(0, 8), -1: slice(8 + lat, 16 + lat)}
+    lane_src = {0: slice(128, 128 + lon), 1: slice(lon, lon + 128), -1: slice(128, 256)}
+    lane_dst = {0: slice(128, 128 + lon), 1: slice(0, 128), -1: slice(128 + lon, 256 + lon)}
+
+    def shell_halo(which):
+        return [
+            send(
+                shell.at[which, row_src[dr], lane_src[dc]],
+                shell.at[which, row_dst[dr], lane_dst[dc]],
+                device,
+            )
+            for (dr, dc), device in compass.items()
+        ]
+
+    loads["sigma"].wait()
+    loads["prior"].wait()
+    shell_copies = shell_halo(slice(0, 2))
 
     per_row = lon // 128
     loads["owner"].wait()
@@ -162,72 +228,6 @@
         return jnp.dot(a.astype(jnp.float32), moved, preferred_element_type=jnp.float32).astype(jnp.int32)
 
     block_at[...] = move(ordered // 64) * 64 + move(ordered % 64)
-
-    for j in range(nj):
-        for name in ("f", "v", "l"):
-            loads[(name, j)].wait()
-    for j in range(nj):
-        grid[nq + 2, j, mid, :] = 0.5 * flags[j].astype(jnp.float32)
-    first = nq - 2
-    fields = slice(first, first + 5)
-    top, bottom = slice(TOP, TOP + 8), slice(TOP + cx - 8, TOP + cx)
-    above, below = slice(TOP - 8, TOP), slice(TOP + cx, TOP + cx + 8)
-    rows = cx // GROUPS
-    wide = lax.broadcasted_iota(jnp.int32, (rows, 128), 1)
-
-    def pack(base, count, width):
-        at_left = jnp.zeros((rows, 128), jnp.float32)
-        at_right = jnp.zeros((rows, 128), jnp.float32)
-        for g in range(GROUPS):
-            here = slice(TOP + g * rows, TOP + (g + 1) * rows)
-            for a in range(count):
-                at = 16 * g + width * a
-                mask = (wide >= at) & (wide < at + width)
-                at_left = jnp.where(mask, pltpu.roll(grid[base + a, 0, here, :], at, 1), at_left)
-                moved = pltpu.roll(grid[base + a, nj - 1, here, :], (at + width) % 128, 1)
-                at_right = jnp.where(mask, moved, at_right)
-        return at_left, at_right
-
-    def unpack(base, count, width, from_left, from_right, take, put, size, group):
-        side = lax.broadcasted_iota(jnp.int32, (size, 128), 1) < 64
-        for a in range(count):
-            at = 16 * group + width * a
-            r = pltpu.roll(from_right[take, :], (128 - at) % 128, 1)
-            l = pltpu.roll(from_left[take, :], (256 - width - at) % 128, 1)
-            grid[base + a, nj, put, :] = jnp.where(side, r, l)
-
-    to_left, to_right = pack(first, 5, 3)
-    packs[0] = to_left
-    packs[1] = to_right
-    pl.semaphore_wait(barrier, len(partners))
-    halo = []
-    halo.append(send(grid.at[fields, 0:nj, bottom, :], grid.at[fields, 0:nj, above, :], (down, col)))
-    halo.append(send(grid.at[fields, 0:nj, top, :], grid.at[fields, 0:nj, below, :], (up, col)))
-    halo.append(send(packs.at[1], edges.at[0], (me, right)))
-    halo.append(send(packs.at[0], edges.at[1], (me, left)))
-    halo.append(send(packs.at[1, rows - 8 : rows, :], corners.at[0], (down, right)))
-    halo.append(send(packs.at[0, rows - 8 : rows, :], corners.at[1], (down, left)))
-    halo.append(send(packs.at[1, 0:8, :], corners.at[2], (up, right)))
-    halo.append(send(packs.at[0, 0:8, :], corners.at[3], (up, left)))
-
-    row_src = {0: slice(8, 8 + lat), 1: slice(lat, lat + 8), -1: slice(8, 16)}
-    row_dst = {0: slice(8, 8 + lat), 1: slice(0, 8), -1: slice(8 + lat, 16 + lat)}
-    lane_src = {0: slice(128, 128 + lon), 1: slice(lon, lon + 128), -1: slice(128, 256)}
-    lane_dst = {0: slice(128, 128 + lon), 1: slice(0, 128), -1: slice(128 + lon, 256 + lon)}
-
-    def shell_halo(which):
-        return [
-            send(
-                shell.at[which, row_src[dr], lane_src[dc]],
-                shell.at[which, row_dst[dr], lane_dst[dc]],
-                device,
-            )
-            for (dr, dc), device in compass.items()
-        ]
-
-    loads["sigma"].wait()
-    loads["prior"].wait()
-    shell_copies = shell_halo(slice(0, 2))
 
     for j in range(nj):
         loads[("o", j)].wait()
@@ -341,6 +341,7 @@
         return (both[:, :128] + both[:, 128:]).reshape(2, xs, sb, 128)
 
     sib_copies, x_copies, z_copies = {}, {}, {}
+    order_x = sorted(x_peer, key=lambda d: -min(d, xs - d))
 
     def for_sibling(n):
         dense_sib[n] = sums(duos[n], 1 - core)
@@ -350,9 +351,12 @@
         dense_own[n] = sums(duos[n], core)
         sib_copies[n].wait_recv()
         dense_own[n] = dense_own[n] + got_sib[n]
-        for d in sorted(x_peer, key=lambda d: -min(d, xs - d)):
-            part = dense_own.at[n, :, lax.rem(at_x + d, xs)]
-            x_copies[n, d] = send(part, got_x.at[n, d - 1], x_peer[d])
+        last = n == len(duos) - 1
+        for h in (slice(0, 1), slice(1, 2)) if last else (slice(0, 2),):
+            for d in order_x:
+                part = dense_own.at[n, h, lax.rem(at_x + d, xs)]
+                copy = send(part, got_x.at[n, d - 1, h], x_peer[d])
+                x_copies.setdefault((n, h.start), []).append(copy)
 
     for_sibling(0)
     for n in range(len(duos)):
@@ -370,9 +374,9 @@
         return carry
 
     def along_z(n):
-        for d in x_peer:
-            x_copies[n, d].wait_recv()
         for h, d in enumerate(duos[n]):
+            for copy in x_copies.get((n, h), []):
+                copy.wait_recv()
             part = dense_own[n, h, at_x]
             for e in x_peer:
                 part = part + got_x[n, e - 1, h]
@@ -424,38 +428,59 @@
     phi = phi[8 : 8 + lat, 128 : 128 + lon]
     out_phi[...] = phi
 
-    def piece(z, x, c):
-        return table.at[pl.ds(pl.multiple_of(sec_of(z, x, c) * sb, sb), sb), :]
+    split = sb // 4 * 3
+
+    def piece(z, x, start=0, size=sb):
+        at = sec_of(z, x, core) * sb + start
+        return table.at[pl.ds(pl.multiple_of(at, sb // 4), size), :]
 
     mine = pl.multiple_of(me * sb, sb)
     for c in range(per_row):
         table[pl.ds(mine + c, lat, stride=per_row), :] = phi[:, c * 128 : (c + 1) * 128]
 
-    from_z, from_x, from_sib = {}, {}, []
-    own = piece(at_z, at_x, core)
+    from_z, from_x, first_rows, last_rows, from_sib = {}, {}, {}, {}, []
+    own = piece(at_z, at_x)
     nearest = sorted(range(1, zs), key=lambda d: min(d, zs - d))
+    for d in nearest[:2]:
+        from_z[d] = send(own, own, z_peer[d])
+    for d in order_x:
+        from_x[d] = send(own, own, x_peer[d])
+    for d in nearest[2:]:
+        from_z[d] = send(own, own, z_peer[d])
+
+    def share(part):
+        from_sib.append(send(part, part, sibling))
+
+    def z_back(d):
+        return lax.rem(at_z + zs - d, zs)
+
+    def x_back(d):
+        return lax.rem(at_x + xs - d, xs)
+
+    share(own)
+
+    def along_x(d):
+        from_z[d].wait_recv()
+        part = piece(z_back(d), at_x, 0, split)
+        for e in order_x:
+            first_rows[d, e] = send(part, part, x_peer[e])
+        share(piece(z_back(d), at_x))
+
+    for d in nearest[:2]:
+        along_x(d)
+    for e in order_x[::-1]:
+        from_x[e].wait_recv()
+        part = piece(at_z, x_back(e), split, sb - split)
+        for d in nearest[::-1]:
+            last_rows[d, e] = send(part, part, z_peer[d])
+        share(piece(at_z, x_back(e)))
+    for d in nearest[2:]:
+        along_x(d)
     for d in nearest:
-        from_z[d] = send(own, own, z_peer[d])
-    steps = [0] + nearest
-    order_x = sorted(x_peer, key=lambda d: -min(d, xs - d))
-
-    def along_x(i):
-        dz = steps[i]
-        if dz:
-            from_z[dz].wait_recv()
-        part = piece(lax.rem(at_z + zs - dz, zs), at_x, core)
-        for dx in order_x:
-            from_x[i, dx] = send(part, part, x_peer[dx])
-        from_sib.append(send(part, part, sibling))
-
-    for i in range(zs):
-        along_x(i)
-    for i in range(zs):
-        for dx in order_x:
-            from_x[i, dx].wait_recv()
-            z = lax.rem(at_z + zs - steps[i], zs)
-            part = piece(z, lax.rem(at_x + xs - dx, xs), core)
-            from_sib.append(send(part, part, sibling))
+        for e in order_x:
+            first_rows[d, e].wait_recv()
+            last_rows[d, e].wait_recv()
+            share(piece(z_back(d), x_back(e)))
     for copy in from_sib:
         copy.wait_recv()
     look_load.wait()
@@ -503,7 +528,7 @@
     dims = (zs, xs, secs, blks, nq, cx, cy, lat, lon)
     f32 = jnp.float32
     rows = cx // GROUPS
-    messages = 12 + 8 + 8 + zs // 2 + zs // 2 * (xs - 1) + 2 * (zs - 1) + zs * (xs - 1) + zs * xs
+    messages = 12 + 8 + 8 + zs // 2 + zs // 2 * (xs - 1) + (xs - 1) + 2 * (zs - 1) + (xs - 1) + 2 * (zs - 1) * (xs - 1) + zs * xs
     any_space = pl.BlockSpec(memory_space=pl.ANY)
     vmem = pl.BlockSpec(memory_space=pltpu.VMEM)
 

time: 71.5 us -> 69.9 us (0.978)
  Pallas kernels: 70.8 us -> 69.2 us
    pallas_call x1, Pallas kernels: 68.5 us -> 66.9 us  [on_device(): pl.pallas_call(body, out_shape=(pltpu.VMEM((nq, nj + 1, cx + PAD, 128), f...]
where the time goes in v5:
time: 69.9 us; the launch traced here: 69.8 us
  Pallas kernels  69.2 us (99%)
    pallas_call x1, Pallas kernels, on_device(): pl.pallas_call(body, out_shape=(pltpu.VMEM((nq, nj + 1, cx + PAD, 128), f...  66.9 us
    pallas_call x1, Pallas kernels, on_device(): pl.pallas_call(write_out, out_shape=(jax.ShapeDtypeStruct(state.shape, f3...  2.26 us

profile of v5, /device:TPU:1, one launch (start us, length us, event | category | flops | bytes accessed | tf_op | source)
XLA Modules:
  0.0 69.8 jit_solution(18307533238194364570)
XLA Ops:
  0.6 66.9 %shard_map.94 = (f32[8,5,296,128]{3,2,1,0:T(8,128)S(1)}, f32[16,512]{1,0:T(8,128)S(1)}, f32[4,256,128]{2,1,0:T(8,128)S(1)}) custom-call(f32[8,256,512]{2,1,0:T(8,128)} %refs_0_.1, f32[2,256,512]{2,1,0:T(8,128)} %refs_1_.1, s32[256,512]{1,0:T(8,128)} %refs_2_.1, f32[16,512]{1,0:T(8,128)} %refs_3_.1, f32[16,512]{1,0:T(8,128)} %refs_4_.1, s32[8,128]{1,0:T(8,128)} %bitcast.2, ...), custom_call_target="tpu_custom_call" | custom-call | tf_op jit(solution)/shard_map/pallas_call | solution.py:538
  67.6 2.3 %shard_map.95 = (f32[8,256,512]{2,1,0:T(8,128)}, f32[16,512]{1,0:T(8,128)}, f32[256,512]{1,0:T(8,128)}) custom-call(f32[8,5,296,128]{3,2,1,0:T(8,128)S(1)} %get-tuple-element.6.fresh, f32[16,512]{1,0:T(8,128)S(1)} %get-tuple-element.7.phi, f32[4,256,128]{2,1,0:T(8,128)S(1)} %get-tuple-element.8.foot), custom_call_target="tpu_custom_call" | custom-call | tf_op jit(solution)/shard_map/pallas_call | solution.py:587

commit v6 on v5

--- a/solution.py
+++ b/solution.py
@@ -384,11 +384,8 @@
             if d:
                 z_copies[d] = send(z_part.at[n, h], got_z.at[d - 1], z_peer[d])
 
-    done = (nq - 2) // 2
-    lax.fori_loop(0, done, other, 0)
+    lax.fori_loop(0, nq - 2, other, 0)
     for n in range(len(duos)):
-        if n == len(duos) - 1:
-            lax.fori_loop(done, nq - 2, other, 0)
         along_z(n)
     source = z_part[len(duos) - 1, 1]
     for d in order[:-1]:
@@ -428,11 +425,11 @@
     phi = phi[8 : 8 + lat, 128 : 128 + lon]
     out_phi[...] = phi
 
-    split = sb // 4 * 3
+    split = sb // 8 * 7
 
     def piece(z, x, start=0, size=sb):
         at = sec_of(z, x, core) * sb + start
-        return table.at[pl.ds(pl.multiple_of(at, sb // 4), size), :]
+        return table.at[pl.ds(pl.multiple_of(at, 8), size), :]
 
     mine = pl.multiple_of(me * sb, sb)
     for c in range(per_row):
@@ -486,14 +483,15 @@
     look_load.wait()
 
     def look_up(k, carry):
-        b = pl.multiple_of(8 * k, 8)
-        for r in range(8):
-            for j in range(nj):
-                at = look_up_at[lax.div(b, 128 // nj), lax.rem(b, 128 // nj) * nj + r * nj + j]
-                foot[j, pl.ds(b + r, 1), :] = table[pl.ds(at, 1), :]
+        b = pl.multiple_of(2 * each * k, 8)
+        for n in range(2):
+            for r in range(each):
+                for j in range(nj):
+                    at = look_up_at[2 * k + n, r * nj + j]
+                    foot[j, pl.ds(b + n * each + r, 1), :] = table[pl.ds(at, 1), :]
         return carry
 
-    lax.fori_loop(0, cx // 8, look_up, 0)
+    lax.fori_loop(0, cx // (2 * each), look_up, 0)
     for copy in sent:
         copy.wait_send()
 

time: 69.9 us -> 69.4 us (level)
  no operation moved by 1% of the time
where the time goes in v6:
time: 69.4 us
  Pallas kernels  68.7 us (99%)
    pallas_call x1, Pallas kernels, on_device(): pl.pallas_call(body, out_shape=(pltpu.VMEM((nq, nj + 1, cx + PAD, 128), f...  66.5 us
    pallas_call x1, Pallas kernels, on_device(): pl.pallas_call(write_out, out_shape=(jax.ShapeDtypeStruct(state.shape, f3...  2.26 us

profile of v6, /device:TPU:1, one launch (start us, length us, event | category | flops | bytes accessed | tf_op | source)
XLA Modules:
  0.0 69.4 jit_solution(2653828926732680024)
XLA Ops:
  0.6 66.5 %shard_map.94 = (f32[8,5,296,128]{3,2,1,0:T(8,128)S(1)}, f32[16,512]{1,0:T(8,128)S(1)}, f32[4,256,128]{2,1,0:T(8,128)S(1)}) custom-call(f32[8,256,512]{2,1,0:T(8,128)} %refs_0_.1, f32[2,256,512]{2,1,0:T(8,128)} %refs_1_.1, s32[256,512]{1,0:T(8,128)} %refs_2_.1, f32[16,512]{1,0:T(8,128)} %refs_3_.1, f32[16,512]{1,0:T(8,128)} %refs_4_.1, s32[8,128]{1,0:T(8,128)} %bitcast.2, ...), custom_call_target="tpu_custom_call" | custom-call | tf_op jit(solution)/shard_map/pallas_call | solution.py:536
  67.1 2.3 %shard_map.95 = (f32[8,256,512]{2,1,0:T(8,128)}, f32[16,512]{1,0:T(8,128)}, f32[256,512]{1,0:T(8,128)}) custom-call(f32[8,5,296,128]{3,2,1,0:T(8,128)S(1)} %get-tuple-element.6.fresh, f32[16,512]{1,0:T(8,128)S(1)} %get-tuple-element.7.phi, f32[4,256,128]{2,1,0:T(8,128)S(1)} %get-tuple-element.8.foot), custom_call_target="tpu_custom_call" | custom-call | tf_op jit(solution)/shard_map/pallas_call | solution.py:585

commit v7 on v6

--- a/solution.py
+++ b/solution.py
@@ -384,9 +384,14 @@
             if d:
                 z_copies[d] = send(z_part.at[n, h], got_z.at[d - 1], z_peer[d])
 
-    lax.fori_loop(0, nq - 2, other, 0)
+    ahead = [nq - 6] + [1] * min(2, len(duos) - 1)
+    done = 0
     for n in range(len(duos)):
+        if n < len(ahead):
+            lax.fori_loop(done, done + ahead[n], other, 0)
+            done += ahead[n]
         along_z(n)
+    lax.fori_loop(done, nq - 3, other, 0)
     source = z_part[len(duos) - 1, 1]
     for d in order[:-1]:
         z_copies[d].wait_recv()
@@ -395,6 +400,7 @@
         at = 128 + 128 * c
         shell[2, 8 : 8 + lat, at : at + 128] = source[c * lat : (c + 1) * lat, :]
     source_copies = shell_halo(slice(2, 3))
+    lax.fori_loop(nq - 3, nq - 2, other, 0)
 
     for copy in shell_copies:
         copy.wait_recv()

time: 69.4 us -> 66.7 us (0.961)
  Pallas kernels: 68.7 us -> 65.8 us
    pallas_call x1, Pallas kernels: 66.5 us -> 63.6 us  [on_device(): pl.pallas_call(body, out_shape=(pltpu.VMEM((nq, nj + 1, cx + PAD, 128), f...]
where the time goes in v7:
time: 66.7 us; the launch traced here: 66.6 us
  Pallas kernels  65.8 us (99%)
  between operations  0.8 us (1%)
    pallas_call x1, Pallas kernels, on_device(): pl.pallas_call(body, out_shape=(pltpu.VMEM((nq, nj + 1, cx + PAD, 128), f...  63.6 us
    pallas_call x1, Pallas kernels, on_device(): pl.pallas_call(write_out, out_shape=(jax.ShapeDtypeStruct(state.shape, f3...  2.26 us

profile of v7, /device:TPU:1, one launch (start us, length us, event | category | flops | bytes accessed | tf_op | source)
XLA Modules:
  0.0 66.6 jit_solution(12511244393495535770)
XLA Ops:
  0.6 63.6 %shard_map.94 = (f32[8,5,296,128]{3,2,1,0:T(8,128)S(1)}, f32[16,512]{1,0:T(8,128)S(1)}, f32[4,256,128]{2,1,0:T(8,128)S(1)}) custom-call(f32[8,256,512]{2,1,0:T(8,128)} %refs_0_.1, f32[2,256,512]{2,1,0:T(8,128)} %refs_1_.1, s32[256,512]{1,0:T(8,128)} %refs_2_.1, f32[16,512]{1,0:T(8,128)} %refs_3_.1, f32[16,512]{1,0:T(8,128)} %refs_4_.1, s32[8,128]{1,0:T(8,128)} %bitcast.2, ...), custom_call_target="tpu_custom_call" | custom-call | tf_op jit(solution)/shard_map/pallas_call | solution.py:542
  64.2 2.3 %shard_map.95 = (f32[8,256,512]{2,1,0:T(8,128)}, f32[16,512]{1,0:T(8,128)}, f32[256,512]{1,0:T(8,128)}) custom-call(f32[8,5,296,128]{3,2,1,0:T(8,128)S(1)} %get-tuple-element.6.fresh, f32[16,512]{1,0:T(8,128)S(1)} %get-tuple-element.7.phi, f32[4,256,128]{2,1,0:T(8,128)S(1)} %get-tuple-element.8.foot), custom_call_target="tpu_custom_call" | custom-call | tf_op jit(solution)/shard_map/pallas_call | solution.py:591

commit v8 on v7

--- a/solution.py
+++ b/solution.py
@@ -88,14 +88,14 @@
     x_peer = {d: (sec_of(at_z, lax.rem(at_x + d, xs), core), col) for d in range(1, xs)}
     z_peer = {d: (sec_of(lax.rem(at_z + d, zs), at_x, core), col) for d in range(1, zs)}
     compass = {
+        (-1, -1): (up, left),
+        (-1, 1): (up, right),
+        (1, -1): (down, left),
+        (1, 1): (down, right),
         (-1, 0): (up, col),
         (1, 0): (down, col),
         (0, -1): (me, left),
         (0, 1): (me, right),
-        (-1, -1): (up, left),
-        (-1, 1): (up, right),
-        (1, -1): (down, left),
-        (1, 1): (down, right),
     }
 
     used = [0]
@@ -117,7 +117,8 @@
         return copy
 
     barrier = pltpu.get_barrier_semaphore()
-    partners = [*compass.values(), *x_peer.values(), *z_peer.values(), sibling]
+    far_z = [z_peer[d] for d in sorted(z_peer, key=lambda d: -min(d, zs - d))]
+    partners = [*far_z, *compass.values(), *x_peer.values(), sibling]
     for device in partners:
         pl.semaphore_signal(barrier, inc=1, device_id=device, device_id_type=MESH)
 
@@ -129,7 +130,8 @@
         loads[name] = copy
 
     mid = slice(TOP, TOP + cx)
-    for j in range(nj):
+    outer, inner = [0, nj - 1], list(range(1, nj - 1))
+    for j in outer + inner:
         lanes = slice(128 * j, 128 * j + 128)
         load(("f", j), state.at[nq - 2 : nq, :, lanes], grid.at[nq - 2 : nq, j, mid, :])
         load(("v", j), velocity.at[:, :, lanes], grid.at[nq : nq + 2, j, mid, :])
@@ -142,11 +144,13 @@
         lanes = slice(128 * j, 128 * j + 128)
         load(("o", j), state.at[: nq - 2, :, lanes], grid.at[: nq - 2, j, mid, :])
 
-    for j in range(nj):
+    def loaded(j):
         for name in ("f", "v", "l"):
             loads[(name, j)].wait()
-    for j in range(nj):
         grid[nq + 2, j, mid, :] = 0.5 * flags[j].astype(jnp.float32)
+
+    for j in outer:
+        loaded(j)
     first = nq - 2
     fields = slice(first, first + 5)
     top, bottom = slice(TOP, TOP + 8), slice(TOP + cx - 8, TOP + cx)
@@ -178,16 +182,18 @@
     to_left, to_right = pack(first, 5, 3)
     packs[0] = to_left
     packs[1] = to_right
+    for j in inner:
+        loaded(j)
     pl.semaphore_wait(barrier, len(partners))
     halo = []
+    halo.append(send(packs.at[1, rows - 8 : rows, :], corners.at[0], (down, right)))
+    halo.append(send(packs.at[0, rows - 8 : rows, :], corners.at[1], (down, left)))
+    halo.append(send(packs.at[1, 0:8, :], corners.at[2], (up, right)))
+    halo.append(send(packs.at[0, 0:8, :], corners.at[3], (up, left)))
     halo.append(send(grid.at[fields, 0:nj, bottom, :], grid.at[fields, 0:nj, above, :], (down, col)))
     halo.append(send(grid.at[fields, 0:nj, top, :], grid.at[fields, 0:nj, below, :], (up, col)))
     halo.append(send(packs.at[1], edges.at[0], (me, right)))
     halo.append(send(packs.at[0], edges.at[1], (me, left)))
-    halo.append(send(packs.at[1, rows - 8 : rows, :], corners.at[0], (down, right)))
-    halo.append(send(packs.at[0, rows - 8 : rows, :], corners.at[1], (down, left)))
-    halo.append(send(packs.at[1, 0:8, :], corners.at[2], (up, right)))
-    halo.append(send(packs.at[0, 0:8, :], corners.at[3], (up, left)))
 
     row_src = {0: slice(8, 8 + lat), 1: slice(lat, lat + 8), -1: slice(8, 16)}
     row_dst = {0: slice(8, 8 + lat), 1: slice(0, 8), -1: slice(8 + lat, 16 + lat)}

time: 66.7 us -> 65.3 us (0.979)
  Pallas kernels: 65.8 us -> 64.4 us
    pallas_call x1, Pallas kernels: 63.6 us -> 62.2 us  [on_device(): pl.pallas_call(body, out_shape=(pltpu.VMEM((nq, nj + 1, cx + PAD, 128), f...]
where the time goes in v8:
time: 65.3 us; the launch traced here: 65.2 us
  Pallas kernels  64.4 us (99%)
  between operations  0.8 us (1%)
    pallas_call x1, Pallas kernels, on_device(): pl.pallas_call(body, out_shape=(pltpu.VMEM((nq, nj + 1, cx + PAD, 128), f...  62.2 us
    pallas_call x1, Pallas kernels, on_device(): pl.pallas_call(write_out, out_shape=(jax.ShapeDtypeStruct(state.shape, f3...  2.26 us

profile of v8, /device:TPU:1, one launch (start us, length us, event | category | flops | bytes accessed | tf_op | source)
XLA Modules:
  0.0 65.2 jit_solution(7170991153906803732)
XLA Ops:
  0.6 62.2 %shard_map.94 = (f32[8,5,296,128]{3,2,1,0:T(8,128)S(1)}, f32[16,512]{1,0:T(8,128)S(1)}, f32[4,256,128]{2,1,0:T(8,128)S(1)}) custom-call(f32[8,256,512]{2,1,0:T(8,128)} %refs_0_.1, f32[2,256,512]{2,1,0:T(8,128)} %refs_1_.1, s32[256,512]{1,0:T(8,128)} %refs_2_.1, f32[16,512]{1,0:T(8,128)} %refs_3_.1, f32[16,512]{1,0:T(8,128)} %refs_4_.1, s32[8,128]{1,0:T(8,128)} %bitcast.2, ...), custom_call_target="tpu_custom_call" | custom-call | tf_op jit(solution)/shard_map/pallas_call | solution.py:548
  62.8 2.3 %shard_map.95 = (f32[8,256,512]{2,1,0:T(8,128)}, f32[16,512]{1,0:T(8,128)}, f32[256,512]{1,0:T(8,128)}) custom-call(f32[8,5,296,128]{3,2,1,0:T(8,128)S(1)} %get-tuple-element.6.fresh, f32[16,512]{1,0:T(8,128)S(1)} %get-tuple-element.7.phi, f32[4,256,128]{2,1,0:T(8,128)S(1)} %get-tuple-element.8.foot), custom_call_target="tpu_custom_call" | custom-call | tf_op jit(solution)/shard_map/pallas_call | solution.py:597

commit v9 on v8

--- a/solution.py
+++ b/solution.py
@@ -304,11 +304,8 @@
             flux_above = speed * jnp.where(speed > 0.0, left_x[j, above, :], right_x[j, at, :])
             fresh[q, j, at, :] = here[j] - ((flux_x - flux_above) + (flux_y - flux_before))
 
-    def field(q, carry):
-        advect(q, nj + 1, TOP - 8, cx + 16)
-        return carry
-
-    lax.fori_loop(nq - 2, nq, field, 0)
+    advect(nq - 2, nj + 1, TOP - 8, cx + 16)
+    advect(nq - 1, nj + 1, TOP - 8, cx + 16)
     lane_c = lax.broadcasted_iota(jnp.int32, (cx, 128), 1)
     field_x = [fresh[nq - 2, j, mid, :] for j in range(nj + 1)]
     after, before = lane_next(field_x, lane_c), lane_prev(field_x, lane_c)
@@ -390,7 +387,7 @@
             if d:
                 z_copies[d] = send(z_part.at[n, h], got_z.at[d - 1], z_peer[d])
 
-    ahead = [nq - 6] + [1] * min(2, len(duos) - 1)
+    ahead = [1, nq - 6, 1][: len(duos)]
     done = 0
     for n in range(len(duos)):
         if n < len(ahead):

time: 65.3 us -> 64.1 us (0.982)
  Pallas kernels: 64.4 us -> 63.2 us
    pallas_call x1, Pallas kernels: 62.2 us -> 61 us  [on_device(): pl.pallas_call(body, out_shape=(pltpu.VMEM((nq, nj + 1, cx + PAD, 128), f...]
where the time goes in v9:
time: 64.1 us; the launch traced here: 64 us
  Pallas kernels  63.2 us (99%)
  between operations  0.8 us (1%)
    pallas_call x1, Pallas kernels, on_device(): pl.pallas_call(body, out_shape=(pltpu.VMEM((nq, nj + 1, cx + PAD, 128), f...  61 us
    pallas_call x1, Pallas kernels, on_device(): pl.pallas_call(write_out, out_shape=(jax.ShapeDtypeStruct(state.shape, f3...  2.26 us

profile of v9, /device:TPU:1, one launch (start us, length us, event | category | flops | bytes accessed | tf_op | source)
XLA Modules:
  0.0 64.0 jit_solution(1704233680689159336)
XLA Ops:
  0.6 61.0 %shard_map.94 = (f32[8,5,296,128]{3,2,1,0:T(8,128)S(1)}, f32[16,512]{1,0:T(8,128)S(1)}, f32[4,256,128]{2,1,0:T(8,128)S(1)}) custom-call(f32[8,256,512]{2,1,0:T(8,128)} %refs_0_.1, f32[2,256,512]{2,1,0:T(8,128)} %refs_1_.1, s32[256,512]{1,0:T(8,128)} %refs_2_.1, f32[16,512]{1,0:T(8,128)} %refs_3_.1, f32[16,512]{1,0:T(8,128)} %refs_4_.1, s32[8,128]{1,0:T(8,128)} %bitcast.2, ...), custom_call_target="tpu_custom_call" | custom-call | tf_op jit(solution)/shard_map/pallas_call | solution.py:545
  61.6 2.3 %shard_map.95 = (f32[8,256,512]{2,1,0:T(8,128)}, f32[16,512]{1,0:T(8,128)}, f32[256,512]{1,0:T(8,128)}) custom-call(f32[8,5,296,128]{3,2,1,0:T(8,128)S(1)} %get-tuple-element.6.fresh, f32[16,512]{1,0:T(8,128)S(1)} %get-tuple-element.7.phi, f32[4,256,128]{2,1,0:T(8,128)S(1)} %get-tuple-element.8.foot), custom_call_target="tpu_custom_call" | custom-call | tf_op jit(solution)/shard_map/pallas_call | solution.py:594
